TPU v7x, 1024 devices: a whole 8x8x8 slice. The times are simulated.
1024 devices in a mesh: dp: 64 (over y, x), expert: 16 (over z, core).
Axes of the slice: x: 8, y: 8, z: 8, core: 2. Of those that a mesh axis runs over, the one named last changes fastest.
Arguments:
- routes: int32 [544, 4], P('expert'), may hold values from 0 to 15, all different within a row; in each aligned block of 34 rows (0 to 33, 34 to 67, ...) at most 10 rows name the same one
- probs: float32 [544, 4], P('expert'), may hold values from 0.05 to 1
- out_grad: bfloat16 [544, 6144], P('expert'), may hold values from -6 to 6
- saved_inputs: bfloat16 [16, 16, 10, 6144], P('expert'), may hold values from -6 to 6
- w_gate: bfloat16 [16, 5376, 6144], P('expert', 'dp'), may hold values from -0.078125 to 0.078125
- w_up: bfloat16 [16, 5376, 6144], P('expert', 'dp'), may hold values from -0.078125 to 0.078125
- w_down: bfloat16 [16, 5376, 6144], P('expert', 'dp'), may hold values from -0.078125 to 0.078125
Outputs:
- in_grad: bfloat16 [544, 6144], P('expert', 'dp')
- prob_grad: float32 [544, 4], P('expert')
Inputs may be any that keep to these rules, and one draw needn't show every extreme that they name: `routes`: each row names 4 different experts; within one block of 34 tokens no expert is named more than 10 times, and in some block some expert is named exactly 10 times.
All inputs are finite; a program needn't handle non-finite values.
Results may differ from a plain program's by a relative error of at most 0.012.
Values may be sent and summed in bfloat16 or wider, within the bound.
No kernel may reach another device: no remote copies, remote signals or barrier semaphores. Data moves between devices by JAX's collectives and lax.ppermute only.
A program may use at most 128 MiB of HBM per device.

v0:
```python
import jax
import jax.numpy as jnp
from jax import lax
from jax.sharding import PartitionSpec as P


def route_slots(flat_routes, experts, capacity):
    one_hot = (flat_routes[:, None] == jnp.arange(experts, dtype=jnp.int32)[None, :]).astype(
        jnp.int32
    )
    before = jnp.cumsum(one_hot, axis=0) - one_hot
    position = jnp.sum(before * one_hot, axis=1)
    return flat_routes * capacity + position


def on_device(routes, probs, out_grad, saved_inputs, w_gate, w_up, w_down):
    experts = lax.axis_size("expert")
    num_tokens = out_grad.shape[0]
    choices_per = routes.shape[1]
    capacity = saved_inputs.shape[2]
    model_width = out_grad.shape[1]
    slot_count = experts * capacity
    contract = (((1,), (1,)), ((), ()))
    flat_routes = routes.reshape(num_tokens * choices_per)
    slot_index = route_slots(flat_routes, experts, capacity)
    selected = slot_index[None, :] == jnp.arange(slot_count, dtype=jnp.int32)[:, None]
    picker = jnp.sum(
        selected.reshape(slot_count, num_tokens, choices_per).astype(jnp.float32), axis=2
    ).astype(jnp.bfloat16)
    send_grads = jnp.dot(picker, out_grad, preferred_element_type=jnp.float32).astype(jnp.bfloat16)
    send_grads = send_grads.reshape(experts, capacity, model_width)
    route_probs = probs.reshape(num_tokens * choices_per).astype(jnp.bfloat16).astype(jnp.float32)
    prob_slots = jnp.sum(jnp.where(selected, route_probs[None, :], 0.0), axis=1).astype(
        jnp.bfloat16
    )
    prob_slots = prob_slots.reshape(experts, capacity)
    inputs = saved_inputs[0].reshape(slot_count, model_width)
    gate_weight = w_gate[0]
    up_weight = w_up[0]
    down_weight = w_down[0]
    gate_pre = lax.dot_general(inputs, gate_weight, contract, preferred_element_type=jnp.float32)
    up_pre = lax.dot_general(inputs, up_weight, contract, preferred_element_type=jnp.float32)
    sigmoid_gate = jax.nn.sigmoid(gate_pre)
    silu_gate = gate_pre * sigmoid_gate
    hidden = (silu_gate * up_pre).astype(jnp.bfloat16)
    column_share = model_width // lax.axis_size("dp")
    recv_grads, recv_probs = (
        lax.all_to_all(send_grads, "expert", split_axis=0, concat_axis=0, tiled=True),
        lax.all_to_all(prob_slots, "expert", split_axis=0, concat_axis=0, tiled=True),
    )
    back = lax.dot_general(
        recv_grads.reshape(slot_count, model_width),
        down_weight,
        contract,
        preferred_element_type=jnp.float32,
    )
    prob_part = jnp.sum(hidden.astype(jnp.float32) * back, axis=1)
    prob_total = lax.psum(prob_part, "dp")
    scaled = recv_probs.reshape(slot_count).astype(jnp.float32)[:, None] * back
    d_gate = (scaled * up_pre * sigmoid_gate * (1.0 + gate_pre * (1.0 - sigmoid_gate))).astype(
        jnp.bfloat16
    )
    d_up = (scaled * silu_gate).astype(jnp.bfloat16)
    across = (((0,), (1,)), ((), ()))
    result = lax.dot_general(gate_weight, d_gate, across, preferred_element_type=jnp.float32)
    summed = lax.psum_scatter(
        result + lax.dot_general(up_weight, d_up, across, preferred_element_type=jnp.float32),
        "dp",
        scatter_dimension=0,
        tiled=True,
    )
    back_cols = summed.astype(jnp.bfloat16).reshape(column_share, experts, capacity)
    prob_back = prob_total.astype(jnp.bfloat16).reshape(1, experts, capacity)
    got_cols, got_probs = (
        lax.all_to_all(back_cols, "expert", split_axis=1, concat_axis=1, tiled=True),
        lax.all_to_all(prob_back, "expert", split_axis=1, concat_axis=1, tiled=True),
    )
    in_grad = lax.dot_general(
        picker,
        got_cols.reshape(column_share, slot_count),
        (((0,), (1,)), ((), ())),
        preferred_element_type=jnp.float32,
    )
    slot_probs = got_probs.reshape(slot_count).astype(jnp.float32)
    prob_grad = jnp.sum(jnp.where(selected, slot_probs[:, None], 0.0), axis=0)
    return (in_grad.astype(jnp.bfloat16), prob_grad.reshape(num_tokens, choices_per))


def solution(mesh):
    placed = (
        P("expert", None),
        P("expert", None),
        P("expert", None),
        P("expert", None, None, None),
        P("expert", "dp", None),
        P("expert", "dp", None),
        P("expert", "dp", None),
    )
    return jax.shard_map(
        on_device,
        mesh=mesh,
        in_specs=placed,
        out_specs=(P("expert", "dp"), P("expert", None)),
        check_vma=False,
    )
```

profile of v0, /device:TPU:1, one launch (start us, length us, event | category | flops | bytes accessed | tf_op | source)
XLA Modules:
  0.0 554.8 jit_solution(9405991874731495808)
XLA Ops:
  7.2 0.0 copy-start
  7.2 0.9 copy.47
  8.0 0.1 eq.42
  8.2 0.6 reduce-window.6
  8.8 0.2 slice_reduce_fusion
  9.0 0.1 bitcast_bitcast_fusion
  9.1 0.1 reduce_sum.48
  9.2 0.1 copy.50
  9.3 0.7 multiply_add_fusion
  10.0 0.1 copy.51
  10.1 0.2 convert_reduce_fusion
  10.3 1.7 convolution_convert_fusion
  12.0 2.5 reshape.97
  14.5 0.0 copy-start.3
  14.5 18.5 %all-to-all-start.1 = ((bf16[16,10,6144]{2,1,0:T(8,128)(2,1)}), bf16[16,10,6144]{2,1,0:T(8,128)(2,1)}, u32[]{:S(2)}, u32[]{:S(2)}) async-start(bf16[16,10,6144]{2,1,0:T(8,128)(2,1)} %reshape.97), calls=%async_computation.1 | async-start | bytes 6291456 | tf_op jit(solution)/shard_map/all_to_all | solution.py:48
  33.0 0.0 copy-done.3
  33.0 2.9 copy.54
  35.9 0.0 copy-start.4
  35.9 3.0 reshape_squeeze.3
  38.9 0.0 copy-done.4
  38.9 0.0 copy-start.1
  38.9 0.0 copy-done
  38.9 0.7 fusion.3
  39.6 0.5 copy-done.1
  40.1 0.7 fusion.6
  40.8 63.4 %all-to-all-done.1 = bf16[16,10,6144]{2,1,0:T(8,128)(2,1)} async-done(((bf16[16,10,6144]{2,1,0:T(8,128)(2,1)}), bf16[16,10,6144]{2,1,0:T(8,128)(2,1)}, u32[]{:S(2)}, u32[]{:S(2)}) %all-to-all-start.1) | async-done | bytes 1966112 | tf_op jit(solution)/shard_map/all_to_all | solution.py:48
  104.1 3.0 reshape.98
  107.1 2.0 multiply_reduce_fusion
  109.1 116.6 %psum.7 = bf16[160]{0:T(256)(128)(2,1)S(1)} all-reduce(f32[160]{0:T(256)S(1)} %get-tuple-element.14), channel_id=1, replica_groups=mesh['dp'=64,'expert'=16] {'dp'}, use_global_device_ids=true, to_apply=%region_7.8 | all-reduce | flops 160 | bytes 960 | tf_op jit(solution)/shard_map/psum | solution.py:58
  225.7 0.7 reshape.107
  226.4 33.1 %all-to-all-start.3 = ((bf16[1,16,10]{2,0,1:T(2,128)(2,1)}), bf16[1,16,10]{2,0,1:T(2,128)(2,1)S(1)}, u32[]{:S(2)}, u32[]{:S(2)}) async-start(bf16[1,16,10]{2,0,1:T(2,128)(2,1)} %reshape.107), calls=%async_computation.3 | async-start | bytes 16384 | tf_op jit(solution)/shard_map/all_to_all | solution.py:76
  259.6 0.0 reduce-scatter.4.cloned.1.call-start
  259.6 0.1 copy.52
  259.7 0.1 reshape.104
  259.8 6.7 %all-to-all-done.3 = bf16[1,16,10]{2,0,1:T(2,128)(2,1)S(1)} async-done(((bf16[1,16,10]{2,0,1:T(2,128)(2,1)}), bf16[1,16,10]{2,0,1:T(2,128)(2,1)S(1)}, u32[]{:S(2)}, u32[]{:S(2)}) %all-to-all-start.3) | async-done | bytes 352 | tf_op jit(solution)/shard_map/all_to_all | solution.py:76
  266.5 0.1 reshape.106
  266.6 0.2 select_reduce_fusion
  266.8 0.1 convert_element_type.109
  266.9 10.1 %all_to_all.21 = bf16[16,1,10]{2,1,0:T(2,128)(2,1)S(1)} all-to-all(bf16[16,1,10]{2,1,0:T(2,128)(2,1)S(1)} %convert_element_type.109), channel_id=1, replica_groups=mesh['dp'=64,'expert'=16] {'expert'}, dimensions={0} | all-to-all | bytes 640 | tf_op jit(solution)/shard_map/all_to_all | solution.py:49
  277.1 0.1 reshape.105
  277.2 0.0 copy-start.2
  277.2 0.7 fusion.1
  277.9 0.5 copy-done.2
  278.4 2.7 fusion
  281.1 6.0 %copy.57 = f32[6144,160]{1,0:T(8,128)} copy(f32[6144,160]{0,1:T(8,128)} %fusion) | data formatting | bytes 7864320
  287.1 0.0 reduce-scatter.4.cloned.1.call-update
  287.1 237.2 %reduce-scatter.4.cloned.1.call-done = f32[96,160]{1,0:T(8,128)} async-done(((f32[6144,160]{1,0:T(8,128)}), f32[96,160]{1,0:T(8,128)}) %reduce-scatter.4.cloned.1.call-update) | async-done | bytes 61456
  524.3 1.0 copy.58
  525.3 0.7 reshape.123
  526.1 13.6 %all-to-all-start.2 = ((bf16[16,2,480]{2,1,0:T(2,128)(2,1)}), bf16[16,2,480]{2,1,0:T(2,128)(2,1)S(1)}, u32[]{:S(2)}, u32[]{:S(2)}) async-start(bf16[16,2,480]{2,1,0:T(2,128)(2,1)} %reshape.123), calls=%async_computation.2 | async-start | bytes 65536 | tf_op jit(solution)/shard_map/all_to_all | solution.py:75
  539.7 0.1 reshape.102
  539.8 0.7 copy.56
  540.5 6.6 %all-to-all-done.2 = bf16[16,2,480]{2,1,0:T(2,128)(2,1)S(1)} async-done(((bf16[16,2,480]{2,1,0:T(2,128)(2,1)}), bf16[16,2,480]{2,1,0:T(2,128)(2,1)S(1)}, u32[]{:S(2)}, u32[]{:S(2)}) %all-to-all-start.2) | async-done | bytes 30752 | tf_op jit(solution)/shard_map/all_to_all | solution.py:75
  547.1 0.1 reshape.124
  547.2 0.7 convolution_convert_fusion.1
  (11 shorter events, 0.2 us)
Async XLA Ops:
  7.2 31.7 %copy-start = (bf16[1,84,6144]{2,1,0:T(8,128)(2,1)S(1)}, bf16[1,84,6144]{2,1,0:T(8,128)(2,1)}, u32[]{:S(2)}) copy-start(bf16[1,84,6144]{2,1,0:T(8,128)(2,1)} %param.11) | copy-start | bytes 3096580
  14.5 18.5 %copy-start.3 = (bf16[1,16,10,6144]{3,1,2,0:T(8,128)(2,1)S(1)}, bf16[1,16,10,6144]{3,1,2,0:T(8,128)(2,1)}, u32[]{:S(2)}) copy-start(bf16[1,16,10,6144]{3,1,2,0:T(8,128)(2,1)} %param.10) | copy-start | bytes 5898244
  14.5 89.7 %all-to-all-start.1 = ((bf16[16,10,6144]{2,1,0:T(8,128)(2,1)}), bf16[16,10,6144]{2,1,0:T(8,128)(2,1)}, u32[]{:S(2)}, u32[]{:S(2)}) async-start(bf16[16,10,6144]{2,1,0:T(8,128)(2,1)} %reshape.97), calls=%async_computation.1 | async-start | bytes 6291456 | tf_op jit(solution)/shard_map/all_to_all | solution.py:48
  35.9 3.0 copy-start.4
  38.9 1.2 copy-start.1
  226.4 40.1 %all-to-all-start.3 = ((bf16[1,16,10]{2,0,1:T(2,128)(2,1)}), bf16[1,16,10]{2,0,1:T(2,128)(2,1)S(1)}, u32[]{:S(2)}, u32[]{:S(2)}) async-start(bf16[1,16,10]{2,0,1:T(2,128)(2,1)} %reshape.107), calls=%async_computation.3 | async-start | bytes 16384 | tf_op jit(solution)/shard_map/all_to_all | solution.py:76
  259.6 264.7 %reduce-scatter.4.cloned.1.call-start = ((), (), s32[]{:S(2)}) async-start(), calls=%async_computation.5 | async-start | bytes 6389760
  277.2 1.2 copy-start.2
  526.1 21.0 %all-to-all-start.2 = ((bf16[16,2,480]{2,1,0:T(2,128)(2,1)}), bf16[16,2,480]{2,1,0:T(2,128)(2,1)S(1)}, u32[]{:S(2)}, u32[]{:S(2)}) async-start(bf16[16,2,480]{2,1,0:T(2,128)(2,1)} %reshape.123), calls=%async_computation.2 | async-start | bytes 65536 | tf_op jit(solution)/shard_map/all_to_all | solution.py:75
Sparse Core Ops, SparseCore 0:
  287.2 237.0 reduce-scatter.3
where the time goes:
time: 556 us; the launch traced here: 555 us
  waiting for transfers between devices  314 us (56%)
  blocking collectives  127 us (23%)
  starting transfers between devices  65.3 us (12%)
  local copies, waits for them, and re-layouts  23.6 us (4%)
  between operations  14.2 us (3%)
  matrix products  9.18 us (2%)
    unnamed x2, waiting for transfers between devices  237 us
    psum x1, blocking collectives, on_device(): prob_total = lax.psum(prob_part, 'dp')  117 us
    all_to_all x1, waiting for transfers between devices, on_device(): lax.all_to_all(send_grads, 'expert', split_axis=0, concat_axis=0, tiled=T...  63.4 us
    all_to_all x1, starting transfers between devices, on_device(): lax.all_to_all(prob_back, 'expert', split_axis=1, concat_axis=1, tiled=True)  33.1 us
    all_to_all x1, starting transfers between devices, on_device(): lax.all_to_all(send_grads, 'expert', split_axis=0, concat_axis=0, tiled=T...  18.5 us
    all_to_all x1, starting transfers between devices, on_device(): lax.all_to_all(back_cols, 'expert', split_axis=1, concat_axis=1, tiled=True)  13.6 us
    unnamed x17, local copies, waits for them, and re-layouts  13.3 us
  transfers between devices with their start and end apart: 4, of which 4 were waited for; matrix products, arithmetic and copies ran while one was open for 1% of the time, Pallas kernels for 0%

commit v1 on v0

v1 whole, which is shorter than its diff:
```python
import jax
import jax.numpy as jnp
from jax import lax
from jax.experimental import pallas as pl
from jax.experimental.pallas import tpu as pltpu
from jax.sharding import Mesh
from jax.sharding import PartitionSpec as P

F32 = jnp.float32
BF16 = jnp.bfloat16
LANES = 128
PAD = 16
SIDE = 8
VMEM_LIMIT = 48 * 1024 * 1024
HELD = jnp.bfloat16


def iota(shape, dim):
    return lax.broadcasted_iota(jnp.int32, shape, dim)


def one_hot(mask):
    return jnp.where(mask, 1.0, 0.0).astype(BF16)


def dot(a, b):
    return jnp.dot(a, b, preferred_element_type=F32)


def params(**more):
    return pltpu.CompilerParams(vmem_limit_bytes=VMEM_LIMIT, **more)


def vmem():
    return pl.BlockSpec(memory_space=pltpu.VMEM)


def pick_kernel(capacity, place, routes, probs, grad_x, grad_y, send, picker):
    rows, tokens = picker.shape
    row = iota((rows, tokens), 0)
    expert, slot = row // PAD, row % PAD
    named = jnp.zeros((rows, tokens), F32)
    weight = jnp.zeros((rows, tokens), F32)
    for k in range(routes.shape[0]):
        hit = routes[k : k + 1, :] == expert
        named = named + jnp.where(hit, 1.0, 0.0)
        weight = weight + jnp.where(hit, probs[k : k + 1, :], 0.0)
    earlier = one_hot(iota((tokens, tokens), 0) < iota((tokens, tokens), 1))
    before = dot(named.astype(BF16), earlier)
    chosen = (named > 0.0) & (before == slot.astype(F32)) & (slot < capacity)
    hot = one_hot(chosen)
    picker[...] = hot
    scale = jnp.sum(jnp.where(chosen, weight, 0.0), axis=1, keepdims=True)
    spread = jnp.where(iota((rows, LANES), 1) == iota((rows, LANES), 0) % PAD, scale, 0.0)
    to_row, from_row = iota((rows, rows), 0), iota((rows, rows), 1)
    gather = one_hot((to_row // PAD == from_row // PAD) & (to_row % PAD == capacity))
    weight_rows = dot(gather, spread.astype(BF16))
    part = grad_x.shape[1]
    even = (iota((rows, part), 0) // PAD) % 2 == 0
    picked = jnp.where(even, dot(hot, grad_x[...]), dot(hot, grad_y[...]))
    send[:, :LANES] = (picked[:, :LANES] + weight_rows).astype(BF16)
    send[:, LANES:] = picked[:, LANES:].astype(BF16)


def pick(place, routes, probs, out_grad, capacity, experts):
    tokens, width = out_grad.shape
    part = width // SIDE
    choices = routes.shape[0]
    rows = experts * PAD
    whole = lambda shape: pl.BlockSpec(shape, lambda i, at: (0, 0))

    def body(*refs):
        pick_kernel(capacity, *refs)

    return pl.pallas_call(
        body,
        grid_spec=pltpu.PrefetchScalarGridSpec(
            num_scalar_prefetch=1,
            grid=(1,),
            in_specs=[
                whole((choices, tokens)),
                whole((choices, tokens)),
                pl.BlockSpec((tokens, part), lambda i, at: (0, at[0])),
                pl.BlockSpec((tokens, part), lambda i, at: (0, at[1])),
            ],
            out_specs=[whole((rows, part)), whole((rows, tokens))],
        ),
        out_shape=[
            jax.ShapeDtypeStruct((rows, part), BF16),
            jax.ShapeDtypeStruct((rows, tokens), BF16),
        ],
        compiler_params=params(),
        name="pick",
    )(place, routes, probs, out_grad, out_grad)


def spread_kernel(capacity, recv, out, scale):
    rows, experts = recv.shape[0], recv.shape[0] // PAD
    slots = experts * capacity
    to_row, from_row = iota((slots, rows), 0), iota((slots, rows), 1)
    first = (to_row % experts) * PAD
    order = one_hot(from_row == first + to_row // experts)
    moved = dot(order, recv[...]).astype(BF16)
    for peer in range(out.shape[0]):
        out[peer] = moved
    weights = dot(one_hot(from_row == first + capacity), recv[:, :LANES])
    own = iota((slots, LANES), 1) == iota((slots, LANES), 0) // experts
    column = jnp.sum(jnp.where(own, weights, 0.0), axis=1, keepdims=True)
    scale[...] = jnp.broadcast_to(column, scale.shape)


def spread(recv, capacity):
    rows, width = recv.shape
    slots = rows // PAD * capacity
    shards = jax.ShapeDtypeStruct((SIDE, slots, width), BF16)

    def body(*refs):
        spread_kernel(capacity, *refs)

    return pl.pallas_call(
        body,
        in_specs=[vmem()],
        out_specs=[vmem()] * 2,
        out_shape=[shards, jax.ShapeDtypeStruct((slots, LANES), F32)],
        compiler_params=params(),
        name="spread",
    )(recv)


def forward_kernel(inputs, w_gate, w_up, gate_pre, up_pre):
    contract = (((1,), (1,)), ((), ()))

    @pl.when(pl.program_id(0) == 0)
    def _():
        gate_pre[...] = jnp.zeros_like(gate_pre)
        up_pre[...] = jnp.zeros_like(up_pre)

    x = inputs[...]
    gate_pre[...] += lax.dot_general(x, w_gate[...], contract, preferred_element_type=F32)
    up_pre[...] += lax.dot_general(x, w_up[...], contract, preferred_element_type=F32)


def forward(inputs, w_gate, w_up):
    slots, width = inputs.shape
    hidden = w_gate.shape[0]
    steps = 4
    piece = lambda rows: pl.BlockSpec((rows, width // steps), lambda i: (0, i))
    whole = pl.BlockSpec((slots, hidden), lambda i: (0, 0))
    shape = jax.ShapeDtypeStruct((slots, hidden), F32)
    return pl.pallas_call(
        forward_kernel,
        grid=(steps,),
        in_specs=[piece(slots), piece(hidden), piece(hidden)],
        out_specs=[whole, whole],
        out_shape=[shape, shape],
        compiler_params=params(),
        cost_estimate=pl.CostEstimate(
            flops=4 * slots * hidden * width,
            bytes_accessed=2 * width * (slots + 2 * hidden),
            transcendentals=0,
        ),
        name="forward",
    )(inputs, w_gate, w_up)


def pack_sums(total):
    high = total.astype(BF16).astype(F32)
    return jnp.where(iota(total.shape, 1) < LANES // 2, high, total - high).astype(BF16)


def unpack_sums(packed):
    return packed + pltpu.roll(packed, LANES // 2, axis=1)


def cut(source, first, width, lane):
    done = 0
    while done < width:
        src, dst = first + done, lane + done
        take = min(width - done, LANES - src % LANES, LANES - dst % LANES)
        shift = (dst - src) % LANES
        values = source(src // LANES)
        if shift:
            values = pltpu.roll(values, shift, axis=1)
        yield dst // LANES, dst % LANES, dst % LANES + take, values
        done += take


def slot_grads_kernel(
    capacity, core, grads, w_down, gate_pre, up_pre, scale, w_gate, w_up, out, held
):
    contract = (((1,), (1,)), ((), ()))
    peers, slots, part = grads.shape
    hidden = w_down.shape[0]
    back = jnp.zeros((slots, hidden), F32)
    for peer in range(peers):
        columns = slice(peer * part, (peer + 1) * part)
        back = back + lax.dot_general(
            grads[peer], w_down[:, columns], contract, preferred_element_type=F32
        )
    gate, up = gate_pre[...], up_pre[...]
    sigmoid_gate = jax.nn.sigmoid(gate)
    silu_gate = gate * sigmoid_gate
    activated = (silu_gate * up).astype(BF16).astype(F32)
    sums = jnp.sum(activated * back, axis=1, keepdims=True)
    scaled = scale[:, :1] * back
    d_gate = (scaled * up * sigmoid_gate * (1.0 + gate * (1.0 - sigmoid_gate))).astype(BF16)
    d_up = (scaled * silu_gate).astype(BF16)

    experts = slots // capacity
    grid = jnp.where(iota((slots, LANES), 1) % (LANES // 2) == iota((slots, LANES), 0) % experts, sums, 0.0)
    rows = [jnp.sum(grid[c * experts : (c + 1) * experts], axis=0, keepdims=True) for c in range(capacity)]
    total = jnp.zeros((PAD, LANES), F32)
    for c, line in enumerate(rows):
        total = jnp.where(iota((PAD, LANES), 0) == c, line, total)
    packed = pack_sums(total)

    block = w_gate.shape[1] // SIDE
    tiles = block // LANES
    share = block // SIDE
    for y in range(SIDE):
        columns = slice(y * block, (y + 1) * block)
        grad = dot(d_gate, w_gate[:, columns]) + dot(d_up, w_up[:, columns])
        held[:, columns] = grad.astype(held.dtype)
    for peer in range(SIDE):
        out[peer, tiles * slots :, :] = packed

    def tile_of(tile):
        return held[:, tile * LANES : (tile + 1) * LANES]

    @pl.when(core[0] == 0)
    def _():
        lane = iota((slots, LANES), 1)
        for x in range(SIDE):
            made = [None] * tiles
            for y in range(SIDE):
                for tile, low, high, values in cut(tile_of, y * block + x * share, share, y * share):
                    if made[tile] is None:
                        made[tile] = values
                    else:
                        made[tile] = jnp.where((lane >= low) & (lane < high), values, made[tile])
            for j in range(tiles):
                out[x, j * slots : (j + 1) * slots, :] = made[j].astype(BF16)

    @pl.when(core[0] == 1)
    def _():
        for y in range(SIDE):
            for j in range(tiles):
                out[y, j * slots : (j + 1) * slots, :] = tile_of(y * tiles + j).astype(BF16)


def slot_grads(core, grads, w_down, gate_pre, up_pre, scale, w_gate, w_up, capacity):
    slots = scale.shape[0]
    width = w_gate.shape[1]
    rows = width // SIDE // LANES * slots + PAD

    def body(*refs):
        slot_grads_kernel(capacity, *refs)

    return pl.pallas_call(
        body,
        in_specs=[pl.BlockSpec(memory_space=pltpu.SMEM)] + [vmem()] * 7,
        out_specs=vmem(),
        out_shape=jax.ShapeDtypeStruct((SIDE, rows, LANES), BF16),
        scratch_shapes=[pltpu.VMEM((slots, width), HELD)],
        compiler_params=params(),
        name="slot_grads",
    )(core, grads, w_down, gate_pre, up_pre, scale, w_gate, w_up)


def total(recv, first, count):
    sums = recv[0, first : first + count].astype(F32)
    for peer in range(1, recv.shape[0]):
        sums = sums + recv[peer, first : first + count].astype(F32)
    return sums


def first_sum_kernel(recv, out):
    peers, rows, _ = recv.shape
    slots = out.shape[1] - PAD
    tiles = (rows - PAD) // slots
    share = tiles * LANES // peers
    columns = [total(recv, j * slots, slots) for j in range(tiles)]
    packed = pack_sums(unpack_sums(total(recv, tiles * slots, PAD)))
    lane = iota((slots, LANES), 1)
    for peer in range(peers):
        made = None
        for _, low, high, values in cut(lambda tile: columns[tile], peer * share, share, 0):
            made = values if made is None else jnp.where((lane >= low) & (lane < high), values, made)
        out[peer, :slots, :] = made.astype(BF16)
        out[peer, slots:, :] = packed


def first_sum(recv, slots):
    return pl.pallas_call(
        first_sum_kernel,
        in_specs=[vmem()],
        out_specs=vmem(),
        out_shape=jax.ShapeDtypeStruct((SIDE, slots + PAD, LANES), BF16),
        compiler_params=params(),
        name="first_sum",
    )(recv)


def second_sum_kernel(share, recv, out):
    slots, rows = recv.shape[1] - PAD, out.shape[0]
    experts = rows // PAD
    grads = total(recv, 0, slots)
    probs = unpack_sums(total(recv, slots, PAD)).astype(BF16)
    line = dot(one_hot(iota((slots, PAD), 0) // experts == iota((slots, PAD), 1)), probs)
    lane, row = iota((slots, LANES), 1), iota((slots, LANES), 0)
    column = jnp.sum(jnp.where(lane == row % experts, line, 0.0), axis=1, keepdims=True)
    values = jnp.where(lane < share, grads, jnp.where(lane == share, column, 0.0)).astype(BF16)
    to_row, from_row = iota((rows, slots), 0), iota((rows, slots), 1)
    order = one_hot(from_row == (to_row % PAD) * experts + to_row // PAD)
    out[...] = dot(order, values).astype(BF16)


def second_sum(recv, share, experts):
    def body(*refs):
        second_sum_kernel(share, *refs)

    return pl.pallas_call(
        body,
        in_specs=[vmem()],
        out_specs=vmem(),
        out_shape=jax.ShapeDtypeStruct((experts * PAD, LANES), BF16),
        compiler_params=params(),
        name="second_sum",
    )(recv)


def combine_kernel(routes, picker, recv, in_grad, prob_grad):
    share = in_grad.shape[1]
    hot, values = picker[...], recv[...]
    summed = lax.dot_general(hot, values, (((0,), (0,)), ((), ())), preferred_element_type=F32)
    in_grad[...] = summed[:, :share].astype(BF16)
    column = values[:, share : share + 1].astype(F32)
    found = jnp.where(hot.astype(F32) > 0.0, column, 0.0)
    expert = iota(hot.shape, 0) // PAD
    for k in range(routes.shape[0]):
        hit = routes[k : k + 1, :] == expert
        prob_grad[k : k + 1, :] = jnp.sum(jnp.where(hit, found, 0.0), axis=0, keepdims=True)


def combine(routes, picker, recv, share):
    choices, tokens = routes.shape
    return pl.pallas_call(
        combine_kernel,
        in_specs=[vmem()] * 3,
        out_specs=[vmem()] * 2,
        out_shape=[
            jax.ShapeDtypeStruct((tokens, share), BF16),
            jax.ShapeDtypeStruct((choices, tokens), F32),
        ],
        compiler_params=params(),
        name="combine",
    )(routes, picker, recv)


def exchange(values):
    return lax.all_to_all(values, "expert", split_axis=0, concat_axis=0, tiled=True)


def exchange_in_plane(values, even_along_x):
    experts = lax.axis_size("expert")
    groups = []
    for expert in range(experts):
        along_x = (expert % 2 == 0) == even_along_x
        for line in range(SIDE):
            group = [(line, i) if along_x else (i, line) for i in range(SIDE)]
            groups.append([(y * SIDE + x) * experts + expert for y, x in group])
    return lax.all_to_all(
        values, ("y", "x", "expert"), split_axis=0, concat_axis=0, axis_index_groups=groups, tiled=True
    )


def on_device(routes, probs, out_grad, saved_inputs, w_gate, w_up, w_down):
    experts = lax.axis_size("expert")
    capacity = saved_inputs.shape[2]
    width = out_grad.shape[1]
    share = width // (SIDE * SIDE)
    slots = experts * capacity
    routes = routes.T
    rounded = probs.T.astype(BF16).astype(F32)
    place = jnp.stack([lax.axis_index("x"), lax.axis_index("y")]).astype(jnp.int32)
    core = (lax.axis_index("expert") % 2).astype(jnp.int32).reshape(1)

    send, picker = pick(place, routes, rounded, out_grad, capacity, experts)
    recv = exchange(send.reshape(experts, PAD, -1)).reshape(experts * PAD, -1)
    inputs = saved_inputs[0].transpose(1, 0, 2).reshape(slots, width)
    gate_pre, up_pre = forward(inputs, w_gate[0], w_up[0])

    shards, scale = spread(recv, capacity)
    grads = exchange_in_plane(shards, True)
    parts = slot_grads(
        core, grads, w_down[0], gate_pre, up_pre, scale, w_gate[0], w_up[0], capacity
    )
    first = first_sum(exchange_in_plane(parts, True), slots)
    back = second_sum(exchange_in_plane(first, False), share, experts)
    got = exchange(back.reshape(experts, PAD, LANES)).reshape(experts * PAD, LANES)
    in_grad, prob_grad = combine(routes, picker, got, share)
    return in_grad, prob_grad.T


def solution(mesh):
    grid = Mesh(mesh.devices.reshape(SIDE, SIDE, -1), ("y", "x", "expert"))
    dp = ("y", "x")
    placed = (
        P("expert", None),
        P("expert", None),
        P("expert", None),
        P("expert", None, None, None),
        P("expert", dp, None),
        P("expert", dp, None),
        P("expert", dp, None),
    )
    return jax.shard_map(
        on_device,
        mesh=grid,
        in_specs=placed,
        out_specs=(P("expert", dp), P("expert", None)),
        check_vma=False,
    )
```

time: 556 us -> 146 us (0.26)
  waiting for transfers between devices: 314 us -> 22.9 us
  starting transfers between devices: 65.3 us -> 7.41 us
  blocking collectives: 127 us -> 95.5 us
  local copies, waits for them, and re-layouts: 23.6 us -> 8.28 us
  between operations: 14.2 us -> 0.69 us
  Pallas kernels: 0 us -> 9.54 us
  matrix products: 9.18 us -> 0 us
    unnamed x2 -> x0, waiting for transfers between devices: 237 us -> none
    psum x1 -> x0, blocking collectives: 117 us -> none  [on_device(): prob_total = lax.psum(prob_part, 'dp')]
    all_to_all x1 -> x4, blocking collectives: 10.1 us -> 95.5 us  [the longest x2 48.1 us: exchange_in_plane(): lax.all_to_all(values, ('y', 'x', 'expert'), split_axis=0, concat_axis=0,...]
    all_to_all x3 -> x1, starting transfers between devices: 65.3 us -> 7.41 us  [exchange_in_plane(): lax.all_to_all(values, ('y', 'x', 'expert'), split_axis=0, concat_axis=0,...]
    all_to_all x3 -> x1, waiting for transfers between devices: 76.7 us -> 22.9 us  [exchange_in_plane(): lax.all_to_all(values, ('y', 'x', 'expert'), split_axis=0, concat_axis=0,...]
    pallas_call x0 -> x7, Pallas kernels: none -> 9.54 us  [the longest x1 4.44 us: slot_grads(): pl.pallas_call(body, in_specs=[pl.BlockSpec(memory_space=pltpu.SMEM)] + [...]
    dot_general x7 -> x0, matrix products: 9.18 us -> none  [the longest x1 2.67 us: on_device(): lax.dot_general(up_weight, d_up, across, preferred_element_type=jnp.float32)]
    reshape x6 -> x0, local copies, waits for them, and re-layouts: 6.28 us -> none  [the longest x1 2.95 us: on_device(): recv_grads.reshape(slot_count, model_width)]
  transfers between devices with their start and end apart: 4 -> 1, of which waited for: 4 -> 1; matrix products, arithmetic and copies ran while one was open for 1% -> 0% of each run, Pallas kernels for 0% -> 1%
where the time goes in v1:
time: 146 us; the launch traced here: 145 us
  blocking collectives  95.5 us (65%)
  waiting for transfers between devices  22.9 us (16%)
  Pallas kernels  9.54 us (7%)
  local copies, waits for them, and re-layouts  8.28 us (6%)
  starting transfers between devices  7.41 us (5%)
    all_to_all x2, blocking collectives, exchange_in_plane(): lax.all_to_all(values, ('y', 'x', 'expert'), split_axis=0, concat_axis=0,...  48.1 us
    all_to_all x2, blocking collectives, exchange(): lax.all_to_all(values, 'expert', split_axis=0, concat_axis=0, tiled=True)  47.4 us
    all_to_all x1, waiting for transfers between devices, exchange_in_plane(): lax.all_to_all(values, ('y', 'x', 'expert'), split_axis=0, concat_axis=0,...  22.9 us
    unnamed x18, local copies, waits for them, and re-layouts  8.28 us
    all_to_all x1, starting transfers between devices, exchange_in_plane(): lax.all_to_all(values, ('y', 'x', 'expert'), split_axis=0, concat_axis=0,...  7.41 us
    pallas_call x1, Pallas kernels, slot_grads(): pl.pallas_call(body, in_specs=[pl.BlockSpec(memory_space=pltpu.SMEM)] + [...  4.44 us
  transfers between devices with their start and end apart: 1, of which 1 were waited for; matrix products, arithmetic and copies ran while one was open for 0% of the time, Pallas kernels for 1%

profile of v1, /device:TPU:1, one launch (start us, length us, event | category | flops | bytes accessed | tf_op | source)
XLA Modules:
  0.0 145.2 jit_solution(2769304539307918262)
XLA Ops:
  0.6 0.7 convert_bitcast_fusion.refs_2_
  1.3 0.1 pad_add_fusion.refs_0_
  1.4 0.0 copy-start.3
  1.4 1.0 copy-done.3
  2.4 0.0 copy-start.7
  2.4 0.7 copy-done.7
  3.1 1.2 pick.1
  4.3 32.5 %all_to_all.25 = bf16[16,16,768]{2,1,0:T(8,128)(2,1)S(1)} all-to-all(bf16[16,16,768]{2,1,0:T(8,128)(2,1)S(1)} %bitcast.26), channel_id=1, replica_groups=mesh['y'=8,'x'=8,'expert'=16] {'expert'}, dimensions={0} | all-to-all | bytes 786432 | tf_op jit(solution)/shard_map/all_to_all | solution.py:361
  36.8 0.3 spread.1
  37.2 0.0 copy-start.5
  37.2 1.3 copy-done.5
  38.5 0.0 copy-start
  38.5 7.4 %all-to-all-start.1 = ((bf16[8,160,768]{2,1,0:T(8,128)(2,1)}), bf16[8,160,768]{2,1,0:T(8,128)(2,1)S(1)}, u32[]{:S(2)}, u32[]{:S(2)}) async-start(bf16[8,160,768]{2,1,0:T(8,128)(2,1)} %copy-done.5), calls=%async_computation.1 | async-start | bytes 3932160 | tf_op jit(solution)/shard_map/all_to_all | solution.py:372
  45.9 0.0 copy-done
  45.9 0.0 copy-start.1
  45.9 1.2 copy-done.1
  47.1 0.0 copy-start.4
  47.1 1.5 %copy-done.4 = bf16[1,16,10,6144]{3,1,2,0:T(8,128)(2,1)S(1)} copy-done((bf16[1,16,10,6144]{3,1,2,0:T(8,128)(2,1)S(1)}, bf16[1,16,10,6144]{3,1,2,0:T(8,128)(2,1)}, u32[]{:S(2)}) %copy-start.4) | copy-done | bytes 1966104
  48.7 2.0 %forward.1 = (f32[160,84]{1,0:T(8,128)S(1)}, f32[160,84]{1,0:T(8,128)S(1)}) custom-call(bf16[160,6144]{1,0:T(8,128)(2,1)S(1)} %bitcast.23, bf16[84,6144]{1,0:T(8,128)(2,1)S(1)} %bitcast.19, bf16[84,6144]{1,0:T(8,128)(2,1)S(1)} %bitcast.21), custom_call_target="tpu_custom_call" | custom-call | flops 330301440 | bytes 4030464 | tf_op jit(solution)/shard_map/forward/pallas_call | solution.py:150
  50.7 22.9 %all-to-all-done.1.refs_1_ = bf16[8,160,768]{2,1,0:T(8,128)(2,1)S(1)} async-done(((bf16[8,160,768]{2,1,0:T(8,128)(2,1)}), bf16[8,160,768]{2,1,0:T(8,128)(2,1)S(1)}, u32[]{:S(2)}, u32[]{:S(2)}) %all-to-all-start.1) | async-done | bytes 1966112 | tf_op jit(solution)/shard_map/all_to_all | solution.py:372
  73.6 0.0 copy-start.2
  73.6 1.2 copy-done.2
  74.9 0.0 copy-start.6
  74.9 1.2 copy-done.6
  76.1 4.4 %slot_grads.1 = bf16[8,976,128]{2,1,0:T(8,128)(2,1)} custom-call(s32[1]{0:T(128)} %bitcast.4.refs_0_, bf16[8,160,768]{2,1,0:T(8,128)(2,1)S(1)} %all-to-all-done.1.refs_1_, bf16[84,6144]{1,0:T(8,128)(2,1)S(1)} %bitcast.25, f32[160,84]{1,0:T(8,128)S(1)} %get-tuple-element.13.refs_3_, f32[160,84]{1,0:T(8,128)S(1)} %get-tuple-element.14.refs_4_, ...), custom_call_target="tpu_custom_call" | custom-call | tf_op jit(solution)/shard_map/slot_grads/pallas_call | solution.py:259
  80.5 31.4 %all_to_all.26.recv = bf16[8,976,128]{2,1,0:T(8,128)(2,1)S(1)} all-to-all(bf16[8,976,128]{2,1,0:T(8,128)(2,1)} %slot_grads.1), channel_id=1, replica_groups={{0,16,32,48,64,80,96,112},{128,144,160,176,192,208,224,240},{256,272,28..., dimensions={0} | all-to-all | bytes 3997696 | tf_op jit(solution)/shard_map/all_to_all | solution.py:372
  112.0 0.0 copy-start.8
  112.0 0.3 first_sum.1
  112.3 16.7 %all_to_all.27.refs_0_ = bf16[8,176,128]{2,1,0:T(8,128)(2,1)S(1)} all-to-all(bf16[8,176,128]{2,1,0:T(8,128)(2,1)S(1)} %first_sum.1), channel_id=1, replica_groups={{0,128,256,384,512,640,768,896},{16,144,272,400,528,656,784,912},{32,16..., dimensions={0} | all-to-all | bytes 720896 | tf_op jit(solution)/shard_map/all_to_all | solution.py:372
  129.0 0.5 second_sum.1
  129.5 14.9 %all_to_all.28 = bf16[16,16,128]{2,1,0:T(8,128)(2,1)S(1)} all-to-all(bf16[16,16,128]{2,1,0:T(8,128)(2,1)S(1)} %bitcast.28), channel_id=1, replica_groups=mesh['y'=8,'x'=8,'expert'=16] {'expert'}, dimensions={0} | all-to-all | bytes 131072 | tf_op jit(solution)/shard_map/all_to_all | solution.py:361
  144.4 0.0 copy-done.8
  144.4 0.8 combine.1
Async XLA Ops:
  1.4 1.0 copy-start.3
  2.4 0.7 copy-start.7
  37.2 1.3 copy-start.5
  38.5 7.4 %copy-start = (bf16[1,84,6144]{2,1,0:T(8,128)(2,1)S(1)}, bf16[1,84,6144]{2,1,0:T(8,128)(2,1)}, u32[]{:S(2)}) copy-start(bf16[1,84,6144]{2,1,0:T(8,128)(2,1)} %param.11) | copy-start | bytes 3096580
  38.5 35.1 %all-to-all-start.1 = ((bf16[8,160,768]{2,1,0:T(8,128)(2,1)}), bf16[8,160,768]{2,1,0:T(8,128)(2,1)S(1)}, u32[]{:S(2)}, u32[]{:S(2)}) async-start(bf16[8,160,768]{2,1,0:T(8,128)(2,1)} %copy-done.5), calls=%async_computation.1 | async-start | bytes 3932160 | tf_op jit(solution)/shard_map/all_to_all | solution.py:372
  45.9 1.2 copy-start.1
  47.1 1.5 %copy-start.4 = (bf16[1,16,10,6144]{3,1,2,0:T(8,128)(2,1)S(1)}, bf16[1,16,10,6144]{3,1,2,0:T(8,128)(2,1)}, u32[]{:S(2)}) copy-start(bf16[1,16,10,6144]{3,1,2,0:T(8,128)(2,1)} %param.10) | copy-start | bytes 5898244
  73.6 1.2 copy-start.2
  74.9 1.2 copy-start.6
  112.0 32.4 %copy-start.8 = (s32[34,4]{0,1:T(4,128)S(1)}, s32[34,4]{0,1:T(4,128)}, u32[]{:S(2)}) copy-start(s32[34,4]{0,1:T(4,128)} %param.7) | copy-start | bytes 1636

commit v2 on v1

--- a/solution.py
+++ b/solution.py
@@ -11,7 +11,7 @@
 LANES = 128
 PAD = 16
 SIDE = 8
-VMEM_LIMIT = 48 * 1024 * 1024
+MIB = 1024 * 1024
 HELD = jnp.bfloat16
 
 
@@ -27,92 +27,137 @@
     return jnp.dot(a, b, preferred_element_type=F32)
 
 
-def params(**more):
-    return pltpu.CompilerParams(vmem_limit_bytes=VMEM_LIMIT, **more)
+def swap(values):
+    row, source = iota((PAD * PAD, PAD * PAD), 0), iota((PAD * PAD, PAD * PAD), 1)
+    order = one_hot(source == (row % PAD) * PAD + row // PAD)
+    return dot(order, values).astype(values.dtype)
+
+
+def params(mib):
+    return pltpu.CompilerParams(vmem_limit_bytes=mib * MIB)
 
 
 def vmem():
     return pl.BlockSpec(memory_space=pltpu.VMEM)
 
 
-def pick_kernel(capacity, place, routes, probs, grad_x, grad_y, send, picker):
-    rows, tokens = picker.shape
-    row = iota((rows, tokens), 0)
-    expert, slot = row // PAD, row % PAD
-    named = jnp.zeros((rows, tokens), F32)
-    weight = jnp.zeros((rows, tokens), F32)
+def hbm():
+    return pl.BlockSpec(memory_space=pltpu.HBM)
+
+
+def smem():
+    return pl.BlockSpec(memory_space=pltpu.SMEM)
+
+
+def pick_kernel(
+    capacity, place, routes_in, probs_in, out_grad, send, picker, routes, probs, grad_x, grad_y, sems
+):
+    slots, tokens = picker.shape
+    experts = slots // capacity
+    tiles = grad_x.shape[1] // LANES
+    copies = [
+        pltpu.make_async_copy(routes_in, routes, sems.at[0]),
+        pltpu.make_async_copy(probs_in, probs, sems.at[1]),
+    ]
+    for axis, grad in enumerate((grad_x, grad_y)):
+        width = grad.shape[1]
+        first = pl.multiple_of(place[axis] * width, LANES)
+        copies.append(
+            pltpu.make_async_copy(out_grad.at[:, pl.ds(first, width)], grad, sems.at[2 + axis])
+        )
+    for copy in copies:
+        copy.start()
+    copies[0].wait()
+    copies[1].wait()
+    row = iota((slots, tokens), 0)
+    expert, slot = row % experts, row // experts
+    named = jnp.zeros((slots, tokens), F32)
+    weight = jnp.zeros((slots, tokens), F32)
+    rounded = probs[...].astype(BF16).astype(F32)
     for k in range(routes.shape[0]):
         hit = routes[k : k + 1, :] == expert
         named = named + jnp.where(hit, 1.0, 0.0)
-        weight = weight + jnp.where(hit, probs[k : k + 1, :], 0.0)
+        weight = weight + jnp.where(hit, rounded[k : k + 1, :], 0.0)
     earlier = one_hot(iota((tokens, tokens), 0) < iota((tokens, tokens), 1))
     before = dot(named.astype(BF16), earlier)
-    chosen = (named > 0.0) & (before == slot.astype(F32)) & (slot < capacity)
+    chosen = (named > 0.0) & (before == slot.astype(F32))
     hot = one_hot(chosen)
     picker[...] = hot
     scale = jnp.sum(jnp.where(chosen, weight, 0.0), axis=1, keepdims=True)
-    spread = jnp.where(iota((rows, LANES), 1) == iota((rows, LANES), 0) % PAD, scale, 0.0)
-    to_row, from_row = iota((rows, rows), 0), iota((rows, rows), 1)
-    gather = one_hot((to_row // PAD == from_row // PAD) & (to_row % PAD == capacity))
-    weight_rows = dot(gather, spread.astype(BF16))
-    part = grad_x.shape[1]
-    even = (iota((rows, part), 0) // PAD) % 2 == 0
-    picked = jnp.where(even, dot(hot, grad_x[...]), dot(hot, grad_y[...]))
-    send[:, :LANES] = (picked[:, :LANES] + weight_rows).astype(BF16)
-    send[:, LANES:] = picked[:, LANES:].astype(BF16)
+    lane = iota((experts, LANES), 1)
+    weights = jnp.zeros((experts, LANES), F32)
+    for c in range(capacity):
+        weights = jnp.where(lane == c, scale[c * experts : (c + 1) * experts], weights)
+    copies[2].wait()
+    copies[3].wait()
+    even = iota((slots, LANES), 0) % 2 == 0
+    pieces = []
+    for j in range(tiles):
+        columns = slice(j * LANES, (j + 1) * LANES)
+        picked = jnp.where(even, dot(hot, grad_x[:, columns]), dot(hot, grad_y[:, columns]))
+        pieces.append(picked.astype(BF16))
+    chunk = send.shape[0] // experts
+    spare = chunk - tiles * capacity - 1
+    pieces += [weights.astype(BF16), jnp.zeros((spare * experts, LANES), BF16)]
+    rows = jnp.concatenate(pieces, axis=0)
+    for g in range(chunk // PAD):
+        group = swap(rows[g * PAD * PAD : (g + 1) * PAD * PAD])
+        for e in range(experts):
+            send[e * chunk + g * PAD : e * chunk + (g + 1) * PAD, :] = group[e * PAD : (e + 1) * PAD]
 
 
 def pick(place, routes, probs, out_grad, capacity, experts):
     tokens, width = out_grad.shape
     part = width // SIDE
     choices = routes.shape[0]
-    rows = experts * PAD
-    whole = lambda shape: pl.BlockSpec(shape, lambda i, at: (0, 0))
+    chunk = -(-(part // LANES * capacity + 1) // PAD) * PAD
 
     def body(*refs):
         pick_kernel(capacity, *refs)
 
     return pl.pallas_call(
         body,
-        grid_spec=pltpu.PrefetchScalarGridSpec(
-            num_scalar_prefetch=1,
-            grid=(1,),
-            in_specs=[
-                whole((choices, tokens)),
-                whole((choices, tokens)),
-                pl.BlockSpec((tokens, part), lambda i, at: (0, at[0])),
-                pl.BlockSpec((tokens, part), lambda i, at: (0, at[1])),
-            ],
-            out_specs=[whole((rows, part)), whole((rows, tokens))],
-        ),
+        in_specs=[smem(), hbm(), hbm(), hbm()],
+        out_specs=[vmem()] * 2,
         out_shape=[
-            jax.ShapeDtypeStruct((rows, part), BF16),
-            jax.ShapeDtypeStruct((rows, tokens), BF16),
+            jax.ShapeDtypeStruct((experts * chunk, LANES), BF16),
+            jax.ShapeDtypeStruct((experts * capacity, tokens), BF16),
         ],
-        compiler_params=params(),
+        scratch_shapes=[
+            pltpu.VMEM((choices, tokens), jnp.int32),
+            pltpu.VMEM((choices, tokens), F32),
+            pltpu.VMEM((tokens, part), BF16),
+            pltpu.VMEM((tokens, part), BF16),
+            pltpu.SemaphoreType.DMA((4,)),
+        ],
+        compiler_params=params(63),
         name="pick",
-    )(place, routes, probs, out_grad, out_grad)
-
-
-def spread_kernel(capacity, recv, out, scale):
-    rows, experts = recv.shape[0], recv.shape[0] // PAD
-    slots = experts * capacity
-    to_row, from_row = iota((slots, rows), 0), iota((slots, rows), 1)
-    first = (to_row % experts) * PAD
-    order = one_hot(from_row == first + to_row // experts)
-    moved = dot(order, recv[...]).astype(BF16)
-    for peer in range(out.shape[0]):
-        out[peer] = moved
-    weights = dot(one_hot(from_row == first + capacity), recv[:, :LANES])
-    own = iota((slots, LANES), 1) == iota((slots, LANES), 0) // experts
-    column = jnp.sum(jnp.where(own, weights, 0.0), axis=1, keepdims=True)
-    scale[...] = jnp.broadcast_to(column, scale.shape)
-
-
-def spread(recv, capacity):
-    rows, width = recv.shape
-    slots = rows // PAD * capacity
-    shards = jax.ShapeDtypeStruct((SIDE, slots, width), BF16)
+    )(place, routes, probs, out_grad)
+
+
+def spread_kernel(capacity, recv, out, scale, held, sems):
+    chunk = recv.shape[0] // PAD
+    moved = []
+    for g in range(chunk // PAD):
+        group = [recv[s * chunk + g * PAD : s * chunk + (g + 1) * PAD, :] for s in range(PAD)]
+        moved.append(swap(jnp.concatenate(group, axis=0)))
+    rows = jnp.concatenate(moved, axis=0)
+    kept = held.shape[0]
+    held[...] = rows[:kept]
+    copies = [pltpu.make_async_copy(held, out.at[i], sems.at[i]) for i in range(out.shape[0])]
+    for copy in copies:
+        copy.start()
+    weights = rows[kept : kept + PAD].astype(F32)
+    for c in range(capacity):
+        column = jnp.broadcast_to(weights[:, c : c + 1], (PAD, LANES))
+        scale[c * PAD : (c + 1) * PAD, :] = column
+    for copy in copies:
+        copy.wait()
+
+
+def spread(recv, part, capacity):
+    slots = PAD * capacity
+    kept = part // LANES * slots
 
     def body(*refs):
         spread_kernel(capacity, *refs)
@@ -120,9 +165,13 @@
     return pl.pallas_call(
         body,
         in_specs=[vmem()],
-        out_specs=[vmem()] * 2,
-        out_shape=[shards, jax.ShapeDtypeStruct((slots, LANES), F32)],
-        compiler_params=params(),
+        out_specs=[hbm(), vmem()],
+        out_shape=[
+            jax.ShapeDtypeStruct((SIDE, kept, LANES), BF16),
+            jax.ShapeDtypeStruct((slots, LANES), F32),
+        ],
+        scratch_shapes=[pltpu.VMEM((kept, LANES), BF16), pltpu.SemaphoreType.DMA((SIDE,))],
+        compiler_params=params(58),
         name="spread",
     )(recv)
 
@@ -153,7 +202,7 @@
         in_specs=[piece(slots), piece(hidden), piece(hidden)],
         out_specs=[whole, whole],
         out_shape=[shape, shape],
-        compiler_params=params(),
+        compiler_params=params(32),
         cost_estimate=pl.CostEstimate(
             flops=4 * slots * hidden * width,
             bytes_accessed=2 * width * (slots + 2 * hidden),
@@ -186,16 +235,24 @@
 
 
 def slot_grads_kernel(
-    capacity, core, grads, w_down, gate_pre, up_pre, scale, w_gate, w_up, out, held
+    capacity, core, grads, down_in, gate_pre, up_pre, scale, gate_in, up_in, out, held, w_down, w_gate, w_up, sems
 ):
+    loads = [
+        pltpu.make_async_copy(source, target, sems.at[i])
+        for i, (source, target) in enumerate(((down_in, w_down), (gate_in, w_gate), (up_in, w_up)))
+    ]
+    for load in loads:
+        load.start()
     contract = (((1,), (1,)), ((), ()))
-    peers, slots, part = grads.shape
-    hidden = w_down.shape[0]
+    peers, slots, hidden = grads.shape[0], scale.shape[0], w_down.shape[0]
+    part = w_down.shape[1] // peers
     back = jnp.zeros((slots, hidden), F32)
+    loads[0].wait()
     for peer in range(peers):
         columns = slice(peer * part, (peer + 1) * part)
+        tiles = [grads[peer, j * slots : (j + 1) * slots, :] for j in range(part // LANES)]
         back = back + lax.dot_general(
-            grads[peer], w_down[:, columns], contract, preferred_element_type=F32
+            jnp.concatenate(tiles, axis=1), w_down[:, columns], contract, preferred_element_type=F32
         )
     gate, up = gate_pre[...], up_pre[...]
     sigmoid_gate = jax.nn.sigmoid(gate)
@@ -217,6 +274,8 @@
     block = w_gate.shape[1] // SIDE
     tiles = block // LANES
     share = block // SIDE
+    loads[1].wait()
+    loads[2].wait()
     for y in range(SIDE):
         columns = slice(y * block, (y + 1) * block)
         grad = dot(d_gate, w_gate[:, columns]) + dot(d_up, w_up[:, columns])
@@ -258,11 +317,15 @@
 
     return pl.pallas_call(
         body,
-        in_specs=[pl.BlockSpec(memory_space=pltpu.SMEM)] + [vmem()] * 7,
+        in_specs=[smem(), vmem(), hbm()] + [vmem()] * 3 + [hbm()] * 2,
         out_specs=vmem(),
         out_shape=jax.ShapeDtypeStruct((SIDE, rows, LANES), BF16),
-        scratch_shapes=[pltpu.VMEM((slots, width), HELD)],
-        compiler_params=params(),
+        scratch_shapes=[
+            pltpu.VMEM((slots, width), HELD),
+            *[pltpu.VMEM(w_down.shape, BF16)] * 3,
+            pltpu.SemaphoreType.DMA((3,)),
+        ],
+        compiler_params=params(58),
         name="slot_grads",
     )(core, grads, w_down, gate_pre, up_pre, scale, w_gate, w_up)
 
@@ -296,7 +359,7 @@
         in_specs=[vmem()],
         out_specs=vmem(),
         out_shape=jax.ShapeDtypeStruct((SIDE, slots + PAD, LANES), BF16),
-        compiler_params=params(),
+        compiler_params=params(32),
         name="first_sum",
     )(recv)
 
@@ -310,9 +373,7 @@
     lane, row = iota((slots, LANES), 1), iota((slots, LANES), 0)
     column = jnp.sum(jnp.where(lane == row % experts, line, 0.0), axis=1, keepdims=True)
     values = jnp.where(lane < share, grads, jnp.where(lane == share, column, 0.0)).astype(BF16)
-    to_row, from_row = iota((rows, slots), 0), iota((rows, slots), 1)
-    order = one_hot(from_row == (to_row % PAD) * experts + to_row // PAD)
-    out[...] = dot(order, values).astype(BF16)
+    out[...] = swap(jnp.concatenate([values, jnp.zeros((rows - slots, LANES), BF16)], axis=0))
 
 
 def second_sum(recv, share, experts):
@@ -324,19 +385,20 @@
         in_specs=[vmem()],
         out_specs=vmem(),
         out_shape=jax.ShapeDtypeStruct((experts * PAD, LANES), BF16),
-        compiler_params=params(),
+        compiler_params=params(32),
         name="second_sum",
     )(recv)
 
 
 def combine_kernel(routes, picker, recv, in_grad, prob_grad):
     share = in_grad.shape[1]
-    hot, values = picker[...], recv[...]
+    hot = picker[...]
+    values = swap(recv[...])[: hot.shape[0]]
     summed = lax.dot_general(hot, values, (((0,), (0,)), ((), ())), preferred_element_type=F32)
     in_grad[...] = summed[:, :share].astype(BF16)
     column = values[:, share : share + 1].astype(F32)
     found = jnp.where(hot.astype(F32) > 0.0, column, 0.0)
-    expert = iota(hot.shape, 0) // PAD
+    expert = iota(hot.shape, 0) % PAD
     for k in range(routes.shape[0]):
         hit = routes[k : k + 1, :] == expert
         prob_grad[k : k + 1, :] = jnp.sum(jnp.where(hit, found, 0.0), axis=0, keepdims=True)
@@ -352,7 +414,7 @@
             jax.ShapeDtypeStruct((tokens, share), BF16),
             jax.ShapeDtypeStruct((choices, tokens), F32),
         ],
-        compiler_params=params(),
+        compiler_params=params(32),
         name="combine",
     )(routes, picker, recv)
 
@@ -381,16 +443,16 @@
     share = width // (SIDE * SIDE)
     slots = experts * capacity
     routes = routes.T
-    rounded = probs.T.astype(BF16).astype(F32)
+    probs = probs.T
     place = jnp.stack([lax.axis_index("x"), lax.axis_index("y")]).astype(jnp.int32)
-    core = (lax.axis_index("expert") % 2).astype(jnp.int32).reshape(1)
-
-    send, picker = pick(place, routes, rounded, out_grad, capacity, experts)
-    recv = exchange(send.reshape(experts, PAD, -1)).reshape(experts * PAD, -1)
+    core = (lax.axis_index("expert") & 1).astype(jnp.int32).reshape(1)
+
+    send, picker = pick(place, routes, probs, out_grad, capacity, experts)
+    recv = exchange(send.reshape(experts, -1, LANES)).reshape(-1, LANES)
     inputs = saved_inputs[0].transpose(1, 0, 2).reshape(slots, width)
     gate_pre, up_pre = forward(inputs, w_gate[0], w_up[0])
 
-    shards, scale = spread(recv, capacity)
+    shards, scale = spread(recv, width // SIDE, capacity)
     grads = exchange_in_plane(shards, True)
     parts = slot_grads(
         core, grads, w_down[0], gate_pre, up_pre, scale, w_gate[0], w_up[0], capacity

time: 146 us -> 145 us (level)
  Pallas kernels: 9.54 us -> 17.2 us
  local copies, waits for them, and re-layouts: 8.28 us -> 2.79 us
  blocking collectives: 95.5 us -> 93.1 us
    pallas_call x3, Pallas kernels: 5.95 us -> 13.5 us  [the longest x1 7.43 us: slot_grads(): pl.pallas_call(body, in_specs=[smem(), vmem(), hbm()] + [vmem()] * 3 + [h...]
    unnamed x18 -> x14, local copies, waits for them, and re-layouts: 8.28 us -> 2.79 us
    all_to_all x2, blocking collectives: 47.4 us -> 44.9 us  [exchange(): lax.all_to_all(values, 'expert', split_axis=0, concat_axis=0, tiled=True)]
where the time goes in v2:
time: 145 us
  blocking collectives  93.1 us (64%)
  waiting for transfers between devices  23 us (16%)
  Pallas kernels  17.2 us (12%)
  starting transfers between devices  7.41 us (5%)
  local copies, waits for them, and re-layouts  2.79 us (2%)
    all_to_all x2, blocking collectives, exchange_in_plane(): lax.all_to_all(values, ('y', 'x', 'expert'), split_axis=0, concat_axis=0,...  48.1 us
    all_to_all x2, blocking collectives, exchange(): lax.all_to_all(values, 'expert', split_axis=0, concat_axis=0, tiled=True)  44.9 us
    all_to_all x1, waiting for transfers between devices, exchange_in_plane(): lax.all_to_all(values, ('y', 'x', 'expert'), split_axis=0, concat_axis=0,...  23 us
    pallas_call x1, Pallas kernels, slot_grads(): pl.pallas_call(body, in_specs=[smem(), vmem(), hbm()] + [vmem()] * 3 + [h...  7.43 us
    all_to_all x1, starting transfers between devices, exchange_in_plane(): lax.all_to_all(values, ('y', 'x', 'expert'), split_axis=0, concat_axis=0,...  7.41 us
    pallas_call x1, Pallas kernels, spread(): pl.pallas_call(body, in_specs=[vmem()], out_specs=[hbm(), vmem()], out_sh...  3.24 us
  transfers between devices with their start and end apart: 1, of which 1 were waited for; matrix products, arithmetic and copies ran while one was open for 0% of the time, Pallas kernels for 1%

profile of v2, /device:TPU:1, one launch (start us, length us, event | category | flops | bytes accessed | tf_op | source)
XLA Modules:
  0.0 144.9 jit_solution(5570556861028514354)
XLA Ops:
  0.6 0.7 pad_add_fusion.refs_0_
  1.3 2.8 %pick.1 = (bf16[1024,128]{1,0:T(8,128)(2,1)}, bf16[160,34]{1,0:T(8,128)(2,1)}) custom-call(s32[2]{0:T(128)} %pad_add_fusion.refs_0_, s32[4,34]{1,0:T(4,128)} %bitcast.25, f32[4,34]{1,0:T(4,128)} %bitcast.30, bf16[34,6144]{1,0:T(8,128)(2,1)} %refs_3_.1), custom_call_target="tpu_custom_call" | custom-call | tf_op jit(solution)/shard_map/pick/pallas_call | solution.py:118
  4.1 30.0 %all_to_all.25 = bf16[16,64,128]{2,1,0:T(8,128)(2,1)} all-to-all(bf16[16,64,128]{2,1,0:T(8,128)(2,1)} %bitcast.29), channel_id=1, replica_groups=mesh['y'=8,'x'=8,'expert'=16] {'expert'}, dimensions={0} | all-to-all | bytes 524288 | tf_op jit(solution)/shard_map/all_to_all | solution.py:423
  34.2 3.2 %spread.1 = (bf16[8,960,128]{2,1,0:T(8,128)(2,1)}, f32[160,128]{1,0:T(8,128)}) custom-call(bf16[1024,128]{1,0:T(8,128)(2,1)} %bitcast.28), custom_call_target="tpu_custom_call" | custom-call | tf_op jit(solution)/shard_map/spread/pallas_call | solution.py:165
  37.4 0.0 copy-start
  37.4 0.0 copy-start.1
  37.4 7.4 %all-to-all-start.1 = ((bf16[8,960,128]{2,1,0:T(8,128)(2,1)}), bf16[8,960,128]{2,1,0:T(8,128)(2,1)}, u32[]{:S(2)}, u32[]{:S(2)}) async-start(bf16[8,960,128]{2,1,0:T(8,128)(2,1)} %get-tuple-element.12), calls=%async_computation.1 | async-start | bytes 3932160 | tf_op jit(solution)/shard_map/all_to_all | solution.py:434
  44.8 0.0 copy-done
  44.8 0.0 copy-done.1
  44.9 0.0 copy-start.2
  44.9 1.5 %copy-done.2 = bf16[1,16,10,6144]{3,1,2,0:T(8,128)(2,1)S(1)} copy-done((bf16[1,16,10,6144]{3,1,2,0:T(8,128)(2,1)S(1)}, bf16[1,16,10,6144]{3,1,2,0:T(8,128)(2,1)}, u32[]{:S(2)}) %copy-start.2) | copy-done | bytes 1966104
  46.4 2.0 %forward.1 = (f32[160,84]{1,0:T(8,128)S(1)}, f32[160,84]{1,0:T(8,128)S(1)}) custom-call(bf16[160,6144]{1,0:T(8,128)(2,1)S(1)} %bitcast.22, bf16[84,6144]{1,0:T(8,128)(2,1)S(1)} %bitcast.19, bf16[84,6144]{1,0:T(8,128)(2,1)S(1)} %bitcast.21), custom_call_target="tpu_custom_call" | custom-call | flops 330301440 | bytes 4030464 | tf_op jit(solution)/shard_map/forward/pallas_call | solution.py:199
  48.4 0.0 copy-start.3
  48.4 0.6 copy-done.3
  49.0 0.0 copy-start.4
  49.0 0.6 copy-done.4
  49.7 23.0 %all-to-all-done.1.refs_1_ = bf16[8,960,128]{2,1,0:T(8,128)(2,1)} async-done(((bf16[8,960,128]{2,1,0:T(8,128)(2,1)}), bf16[8,960,128]{2,1,0:T(8,128)(2,1)}, u32[]{:S(2)}, u32[]{:S(2)}) %all-to-all-start.1) | async-done | bytes 1966112 | tf_op jit(solution)/shard_map/all_to_all | solution.py:434
  72.7 7.4 %slot_grads.1 = bf16[8,976,128]{2,1,0:T(8,128)(2,1)} custom-call(s32[1]{0:T(128)} %bitcast.4.refs_0_, bf16[8,960,128]{2,1,0:T(8,128)(2,1)} %all-to-all-done.1.refs_1_, bf16[84,6144]{1,0:T(8,128)(2,1)} %bitcast.27, f32[160,84]{1,0:T(8,128)} %copy-done.3, f32[160,84]{1,0:T(8,128)} %copy-done.4, f32[160,128]{1,0:T(8,128)} %get-tuple-element.15.refs_5_, ...), custom_call_target="tpu_custom_call" | custom-call | tf_op jit(solution)/shard_map/slot_grads/pallas_call | solution.py:318
  80.1 31.5 %all_to_all.26.recv = bf16[8,976,128]{2,1,0:T(8,128)(2,1)S(1)} all-to-all(bf16[8,976,128]{2,1,0:T(8,128)(2,1)} %slot_grads.1), channel_id=1, replica_groups={{0,16,32,48,64,80,96,112},{128,144,160,176,192,208,224,240},{256,272,28..., dimensions={0} | all-to-all | bytes 3997696 | tf_op jit(solution)/shard_map/all_to_all | solution.py:434
  111.6 0.0 copy-start.5
  111.6 0.0 copy-start.6
  111.6 0.3 first_sum.1
  111.9 16.7 %all_to_all.27.refs_0_ = bf16[8,176,128]{2,1,0:T(8,128)(2,1)S(1)} all-to-all(bf16[8,176,128]{2,1,0:T(8,128)(2,1)S(1)} %first_sum.1), channel_id=1, replica_groups={{0,128,256,384,512,640,768,896},{16,144,272,400,528,656,784,912},{32,16..., dimensions={0} | all-to-all | bytes 720896 | tf_op jit(solution)/shard_map/all_to_all | solution.py:434
  128.6 0.5 second_sum.1
  129.0 14.9 %all_to_all.28 = bf16[16,16,128]{2,1,0:T(8,128)(2,1)S(1)} all-to-all(bf16[16,16,128]{2,1,0:T(8,128)(2,1)S(1)} %bitcast.24), channel_id=1, replica_groups=mesh['y'=8,'x'=8,'expert'=16] {'expert'}, dimensions={0} | all-to-all | bytes 131072 | tf_op jit(solution)/shard_map/all_to_all | solution.py:423
  144.0 0.0 copy-done.5
  144.0 0.0 copy-done.6
  144.0 0.9 combine.1
Async XLA Ops:
  37.4 7.4 %copy-start = (bf16[1,84,6144]{2,1,0:T(8,128)(2,1)S(1)}, bf16[1,84,6144]{2,1,0:T(8,128)(2,1)}, u32[]{:S(2)}) copy-start(bf16[1,84,6144]{2,1,0:T(8,128)(2,1)} %param.11) | copy-start | bytes 3096580
  37.4 7.4 %copy-start.1 = (bf16[1,84,6144]{2,1,0:T(8,128)(2,1)S(1)}, bf16[1,84,6144]{2,1,0:T(8,128)(2,1)}, u32[]{:S(2)}) copy-start(bf16[1,84,6144]{2,1,0:T(8,128)(2,1)} %param.12) | copy-start | bytes 3096580
  37.4 35.2 %all-to-all-start.1 = ((bf16[8,960,128]{2,1,0:T(8,128)(2,1)}), bf16[8,960,128]{2,1,0:T(8,128)(2,1)}, u32[]{:S(2)}, u32[]{:S(2)}) async-start(bf16[8,960,128]{2,1,0:T(8,128)(2,1)} %get-tuple-element.12), calls=%async_computation.1 | async-start | bytes 3932160 | tf_op jit(solution)/shard_map/all_to_all | solution.py:434
  44.9 1.5 %copy-start.2 = (bf16[1,16,10,6144]{3,1,2,0:T(8,128)(2,1)S(1)}, bf16[1,16,10,6144]{3,1,2,0:T(8,128)(2,1)}, u32[]{:S(2)}) copy-start(bf16[1,16,10,6144]{3,1,2,0:T(8,128)(2,1)} %param.10) | copy-start | bytes 5898244
  48.4 0.6 copy-start.3
  49.0 0.6 copy-start.4
  111.6 32.4 %copy-start.5 = (bf16[160,34]{1,0:T(8,128)(2,1)S(1)}, bf16[160,34]{1,0:T(8,128)(2,1)}, u32[]{:S(2)}) copy-start(bf16[160,34]{1,0:T(8,128)(2,1)} %get-tuple-element.10.picker) | copy-start | bytes 32644
  111.6 32.4 %copy-start.6 = (s32[34,4]{0,1:T(4,128)S(1)}, s32[34,4]{0,1:T(4,128)}, u32[]{:S(2)}) copy-start(s32[34,4]{0,1:T(4,128)} %param.7) | copy-start | bytes 1636

commit v3 on v2

--- a/solution.py
+++ b/solution.py
@@ -50,7 +50,7 @@
 
 
 def pick_kernel(
-    capacity, place, routes_in, probs_in, out_grad, send, picker, routes, probs, grad_x, grad_y, sems
+    capacity, at_x, at_y, routes_in, probs_in, out_grad, send, picker, routes, probs, grad_x, grad_y, sems
 ):
     slots, tokens = picker.shape
     experts = slots // capacity
@@ -59,9 +59,9 @@
         pltpu.make_async_copy(routes_in, routes, sems.at[0]),
         pltpu.make_async_copy(probs_in, probs, sems.at[1]),
     ]
-    for axis, grad in enumerate((grad_x, grad_y)):
+    for axis, (at, grad) in enumerate(((at_x, grad_x), (at_y, grad_y))):
         width = grad.shape[1]
-        first = pl.multiple_of(place[axis] * width, LANES)
+        first = pl.multiple_of(at[0] * width, LANES)
         copies.append(
             pltpu.make_async_copy(out_grad.at[:, pl.ds(first, width)], grad, sems.at[2 + axis])
         )
@@ -106,7 +106,7 @@
             send[e * chunk + g * PAD : e * chunk + (g + 1) * PAD, :] = group[e * PAD : (e + 1) * PAD]
 
 
-def pick(place, routes, probs, out_grad, capacity, experts):
+def pick(at_x, at_y, routes, probs, out_grad, capacity, experts):
     tokens, width = out_grad.shape
     part = width // SIDE
     choices = routes.shape[0]
@@ -117,7 +117,7 @@
 
     return pl.pallas_call(
         body,
-        in_specs=[smem(), hbm(), hbm(), hbm()],
+        in_specs=[smem(), smem(), hbm(), hbm(), hbm()],
         out_specs=[vmem()] * 2,
         out_shape=[
             jax.ShapeDtypeStruct((experts * chunk, LANES), BF16),
@@ -132,30 +132,26 @@
         ],
         compiler_params=params(63),
         name="pick",
-    )(place, routes, probs, out_grad)
-
-
-def spread_kernel(capacity, recv, out, scale, held, sems):
+    )(at_x, at_y, routes, probs, out_grad)
+
+
+def spread_kernel(capacity, recv, after, out, scale):
     chunk = recv.shape[0] // PAD
     moved = []
     for g in range(chunk // PAD):
         group = [recv[s * chunk + g * PAD : s * chunk + (g + 1) * PAD, :] for s in range(PAD)]
         moved.append(swap(jnp.concatenate(group, axis=0)))
     rows = jnp.concatenate(moved, axis=0)
-    kept = held.shape[0]
-    held[...] = rows[:kept]
-    copies = [pltpu.make_async_copy(held, out.at[i], sems.at[i]) for i in range(out.shape[0])]
-    for copy in copies:
-        copy.start()
+    kept = out.shape[1]
+    for peer in range(out.shape[0]):
+        out[peer] = rows[:kept]
     weights = rows[kept : kept + PAD].astype(F32)
     for c in range(capacity):
         column = jnp.broadcast_to(weights[:, c : c + 1], (PAD, LANES))
         scale[c * PAD : (c + 1) * PAD, :] = column
-    for copy in copies:
-        copy.wait()
-
-
-def spread(recv, part, capacity):
+
+
+def spread(recv, after, part, capacity):
     slots = PAD * capacity
     kept = part // LANES * slots
 
@@ -164,52 +160,74 @@
 
     return pl.pallas_call(
         body,
-        in_specs=[vmem()],
-        out_specs=[hbm(), vmem()],
+        in_specs=[vmem(), hbm()],
+        out_specs=[vmem(), vmem()],
         out_shape=[
             jax.ShapeDtypeStruct((SIDE, kept, LANES), BF16),
             jax.ShapeDtypeStruct((slots, LANES), F32),
         ],
-        scratch_shapes=[pltpu.VMEM((kept, LANES), BF16), pltpu.SemaphoreType.DMA((SIDE,))],
-        compiler_params=params(58),
+        compiler_params=params(32),
         name="spread",
-    )(recv)
-
-
-def forward_kernel(inputs, w_gate, w_up, gate_pre, up_pre):
+    )(recv, after)
+
+
+def forward_kernel(inputs, gate_in, up_in, down_in, both, down, activated, by_gate, by_up, pre):
     contract = (((1,), (1,)), ((), ()))
-
-    @pl.when(pl.program_id(0) == 0)
+    hidden, pad = gate_in.shape[0], down.shape[0]
+    step = pl.program_id(0)
+    zeros = jnp.zeros((pad - hidden, gate_in.shape[1]), BF16)
+    weights = jnp.concatenate([gate_in[...], zeros, up_in[...], zeros], axis=0)
+    both[...] = weights
+    down[...] = jnp.concatenate([down_in[...], zeros], axis=0)
+    part = lax.dot_general(inputs[...], weights, contract, preferred_element_type=F32)
+
+    @pl.when(step == 0)
     def _():
-        gate_pre[...] = jnp.zeros_like(gate_pre)
-        up_pre[...] = jnp.zeros_like(up_pre)
-
-    x = inputs[...]
-    gate_pre[...] += lax.dot_general(x, w_gate[...], contract, preferred_element_type=F32)
-    up_pre[...] += lax.dot_general(x, w_up[...], contract, preferred_element_type=F32)
-
-
-def forward(inputs, w_gate, w_up):
+        pre[...] = part
+
+    @pl.when(step > 0)
+    def _():
+        pre[...] += part
+
+    @pl.when(step == pl.num_programs(0) - 1)
+    def _():
+        gate, up = pre[:, :pad], pre[:, pad:]
+        sigmoid_gate = jax.nn.sigmoid(gate)
+        silu_gate = gate * sigmoid_gate
+        activated[...] = (silu_gate * up).astype(BF16).astype(F32)
+        by_gate[...] = up * sigmoid_gate * (1.0 + gate * (1.0 - sigmoid_gate))
+        by_up[...] = silu_gate
+
+
+def forward(inputs, w_gate, w_up, w_down):
     slots, width = inputs.shape
     hidden = w_gate.shape[0]
+    pad = -(-hidden // 32) * 32
     steps = 4
     piece = lambda rows: pl.BlockSpec((rows, width // steps), lambda i: (0, i))
-    whole = pl.BlockSpec((slots, hidden), lambda i: (0, 0))
-    shape = jax.ShapeDtypeStruct((slots, hidden), F32)
+    factors = pl.BlockSpec((slots, pad), lambda i: (0, 0))
+    shape = jax.ShapeDtypeStruct((slots, pad), F32)
     return pl.pallas_call(
         forward_kernel,
         grid=(steps,),
-        in_specs=[piece(slots), piece(hidden), piece(hidden)],
-        out_specs=[whole, whole],
-        out_shape=[shape, shape],
+        in_specs=[piece(slots), piece(hidden), piece(hidden), piece(hidden)],
+        out_specs=[piece(2 * pad), piece(pad), factors, factors, factors],
+        out_shape=[
+            jax.ShapeDtypeStruct((2 * pad, width), BF16),
+            jax.ShapeDtypeStruct((pad, width), BF16),
+            shape,
+            shape,
+            shape,
+        ],
+        scratch_shapes=[pltpu.VMEM((slots, 2 * pad), F32)],
         compiler_params=params(32),
         cost_estimate=pl.CostEstimate(
             flops=4 * slots * hidden * width,
-            bytes_accessed=2 * width * (slots + 2 * hidden),
+            bytes_accessed=4 * width * (slots + 3 * hidden),
             transcendentals=0,
         ),
         name="forward",
-    )(inputs, w_gate, w_up)
+    )(inputs, w_gate, w_up, w_down)
 
 
 def pack_sums(total):
@@ -235,33 +253,22 @@
 
 
 def slot_grads_kernel(
-    capacity, core, grads, down_in, gate_pre, up_pre, scale, gate_in, up_in, out, held, w_down, w_gate, w_up, sems
+    capacity, expert, grads, down, activated, by_gate, by_up, scale, both, out, held
 ):
-    loads = [
-        pltpu.make_async_copy(source, target, sems.at[i])
-        for i, (source, target) in enumerate(((down_in, w_down), (gate_in, w_gate), (up_in, w_up)))
-    ]
-    for load in loads:
-        load.start()
     contract = (((1,), (1,)), ((), ()))
-    peers, slots, hidden = grads.shape[0], scale.shape[0], w_down.shape[0]
-    part = w_down.shape[1] // peers
-    back = jnp.zeros((slots, hidden), F32)
-    loads[0].wait()
+    peers, slots, pad = grads.shape[0], scale.shape[0], down.shape[0]
+    part = down.shape[1] // peers
+    back = jnp.zeros((slots, pad), F32)
     for peer in range(peers):
         columns = slice(peer * part, (peer + 1) * part)
         tiles = [grads[peer, j * slots : (j + 1) * slots, :] for j in range(part // LANES)]
         back = back + lax.dot_general(
-            jnp.concatenate(tiles, axis=1), w_down[:, columns], contract, preferred_element_type=F32
+            jnp.concatenate(tiles, axis=1), down[:, columns], contract, preferred_element_type=F32
         )
-    gate, up = gate_pre[...], up_pre[...]
-    sigmoid_gate = jax.nn.sigmoid(gate)
-    silu_gate = gate * sigmoid_gate
-    activated = (silu_gate * up).astype(BF16).astype(F32)
-    sums = jnp.sum(activated * back, axis=1, keepdims=True)
+    sums = jnp.sum(activated[...] * back, axis=1, keepdims=True)
     scaled = scale[:, :1] * back
-    d_gate = (scaled * up * sigmoid_gate * (1.0 + gate * (1.0 - sigmoid_gate))).astype(BF16)
-    d_up = (scaled * silu_gate).astype(BF16)
+    d_gate, d_up = (scaled * by_gate[...]).astype(BF16), (scaled * by_up[...]).astype(BF16)
+    d_both = jnp.concatenate([d_gate, d_up], axis=1)
 
     experts = slots // capacity
     grid = jnp.where(iota((slots, LANES), 1) % (LANES // 2) == iota((slots, LANES), 0) % experts, sums, 0.0)
@@ -271,22 +278,19 @@
         total = jnp.where(iota((PAD, LANES), 0) == c, line, total)
     packed = pack_sums(total)
 
-    block = w_gate.shape[1] // SIDE
+    block = both.shape[1] // SIDE
     tiles = block // LANES
     share = block // SIDE
-    loads[1].wait()
-    loads[2].wait()
     for y in range(SIDE):
         columns = slice(y * block, (y + 1) * block)
-        grad = dot(d_gate, w_gate[:, columns]) + dot(d_up, w_up[:, columns])
-        held[:, columns] = grad.astype(held.dtype)
+        held[:, columns] = dot(d_both, both[:, columns]).astype(held.dtype)
     for peer in range(SIDE):
         out[peer, tiles * slots :, :] = packed
 
     def tile_of(tile):
         return held[:, tile * LANES : (tile + 1) * LANES]
 
-    @pl.when(core[0] == 0)
+    @pl.when(expert[0] % 2 == 0)
     def _():
         lane = iota((slots, LANES), 1)
         for x in range(SIDE):
@@ -300,16 +304,16 @@
             for j in range(tiles):
                 out[x, j * slots : (j + 1) * slots, :] = made[j].astype(BF16)
 
-    @pl.when(core[0] == 1)
+    @pl.when(expert[0] % 2 == 1)
     def _():
         for y in range(SIDE):
             for j in range(tiles):
                 out[y, j * slots : (j + 1) * slots, :] = tile_of(y * tiles + j).astype(BF16)
 
 
-def slot_grads(core, grads, w_down, gate_pre, up_pre, scale, w_gate, w_up, capacity):
+def slot_grads(expert, grads, down, activated, by_gate, by_up, scale, both, capacity):
     slots = scale.shape[0]
-    width = w_gate.shape[1]
+    width = both.shape[1]
     rows = width // SIDE // LANES * slots + PAD
 
     def body(*refs):
@@ -317,17 +321,13 @@
 
     return pl.pallas_call(
         body,
-        in_specs=[smem(), vmem(), hbm()] + [vmem()] * 3 + [hbm()] * 2,
+        in_specs=[smem()] + [vmem()] * 7,
         out_specs=vmem(),
         out_shape=jax.ShapeDtypeStruct((SIDE, rows, LANES), BF16),
-        scratch_shapes=[
-            pltpu.VMEM((slots, width), HELD),
-            *[pltpu.VMEM(w_down.shape, BF16)] * 3,
-            pltpu.SemaphoreType.DMA((3,)),
-        ],
-        compiler_params=params(58),
+        scratch_shapes=[pltpu.VMEM((slots, width), HELD)],
+        compiler_params=params(32),
         name="slot_grads",
-    )(core, grads, w_down, gate_pre, up_pre, scale, w_gate, w_up)
+    )(expert, grads, down, activated, by_gate, by_up, scale, both)
 
 
 def total(recv, first, count):
@@ -444,19 +444,18 @@
     slots = experts * capacity
     routes = routes.T
     probs = probs.T
-    place = jnp.stack([lax.axis_index("x"), lax.axis_index("y")]).astype(jnp.int32)
-    core = (lax.axis_index("expert") & 1).astype(jnp.int32).reshape(1)
-
-    send, picker = pick(place, routes, probs, out_grad, capacity, experts)
+    at_x, at_y, expert = (
+        lax.axis_index(axis).astype(jnp.int32).reshape(1) for axis in ("x", "y", "expert")
+    )
+
+    send, picker = pick(at_x, at_y, routes, probs, out_grad, capacity, experts)
     recv = exchange(send.reshape(experts, -1, LANES)).reshape(-1, LANES)
     inputs = saved_inputs[0].transpose(1, 0, 2).reshape(slots, width)
-    gate_pre, up_pre = forward(inputs, w_gate[0], w_up[0])
-
-    shards, scale = spread(recv, width // SIDE, capacity)
+    both, down, activated, by_gate, by_up = forward(inputs, w_gate[0], w_up[0], w_down[0])
+
+    shards, scale = spread(recv, activated, width // SIDE, capacity)
     grads = exchange_in_plane(shards, True)
-    parts = slot_grads(
-        core, grads, w_down[0], gate_pre, up_pre, scale, w_gate[0], w_up[0], capacity
-    )
+    parts = slot_grads(expert, grads, down, activated, by_gate, by_up, scale, both, capacity)
     first = first_sum(exchange_in_plane(parts, True), slots)
     back = second_sum(exchange_in_plane(first, False), share, experts)
     got = exchange(back.reshape(experts, PAD, LANES)).reshape(experts * PAD, LANES)

time: 145 us -> 140 us (0.966)
  blocking collectives: 93.1 us -> 63.7 us
  starting transfers between devices: 7.41 us -> 25.5 us
  Pallas kernels: 17.2 us -> 9.39 us
  waiting for transfers between devices: 23 us -> 30.3 us
  local copies, waits for them, and re-layouts: 2.79 us -> 9.61 us
    all_to_all x2 -> x1, blocking collectives: 44.9 us -> 16.7 us  [exchange(): lax.all_to_all(values, 'expert', split_axis=0, concat_axis=0, tiled=True)]
    all_to_all x0 -> x1, starting transfers between devices: none -> 18.2 us  [exchange(): lax.all_to_all(values, 'expert', split_axis=0, concat_axis=0, tiled=True)]
    pallas_call x3, Pallas kernels: 13.5 us -> 5.28 us  [the longest x1 2.7 us: slot_grads(): pl.pallas_call(body, in_specs=[smem()] + [vmem()] * 7, out_specs=vmem(),...]
    unnamed x14 -> x18, local copies, waits for them, and re-layouts: 2.79 us -> 9.61 us
    all_to_all x1, waiting for transfers between devices: 23 us -> 27.7 us  [exchange_in_plane(): lax.all_to_all(values, ('y', 'x', 'expert'), split_axis=0, concat_axis=0,...]
    all_to_all x0 -> x1, waiting for transfers between devices: none -> 2.59 us  [exchange(): lax.all_to_all(values, 'expert', split_axis=0, concat_axis=0, tiled=True)]
  transfers between devices with their start and end apart: 1 -> 2, of which waited for: 1 -> 2; matrix products, arithmetic and copies ran while one was open for 0% -> 0% of each run, Pallas kernels for 1% -> 2%
where the time goes in v3:
time: 140 us; the launch traced here: 139 us
  blocking collectives  63.7 us (46%)
  waiting for transfers between devices  30.3 us (22%)
  starting transfers between devices  25.5 us (18%)
  local copies, waits for them, and re-layouts  9.61 us (7%)
  Pallas kernels  9.39 us (7%)
    all_to_all x2, blocking collectives, exchange_in_plane(): lax.all_to_all(values, ('y', 'x', 'expert'), split_axis=0, concat_axis=0,...  47 us
    all_to_all x1, waiting for transfers between devices, exchange_in_plane(): lax.all_to_all(values, ('y', 'x', 'expert'), split_axis=0, concat_axis=0,...  27.7 us
    all_to_all x1, starting transfers between devices, exchange(): lax.all_to_all(values, 'expert', split_axis=0, concat_axis=0, tiled=True)  18.2 us
    all_to_all x1, blocking collectives, exchange(): lax.all_to_all(values, 'expert', split_axis=0, concat_axis=0, tiled=True)  16.7 us
    unnamed x18, local copies, waits for them, and re-layouts  9.61 us
    all_to_all x1, starting transfers between devices, exchange_in_plane(): lax.all_to_all(values, ('y', 'x', 'expert'), split_axis=0, concat_axis=0,...  7.27 us
  transfers between devices with their start and end apart: 2, of which 2 were waited for; matrix products, arithmetic and copies ran while one was open for 0% of the time, Pallas kernels for 2%

profile of v3, /device:TPU:1, one launch (start us, length us, event | category | flops | bytes accessed | tf_op | source)
XLA Modules:
  0.0 139.2 jit_solution(7260563437329809862)
XLA Ops:
  0.6 2.2 %pick.1 = (bf16[1024,128]{1,0:T(8,128)(2,1)}, bf16[160,34]{1,0:T(8,128)(2,1)}) custom-call(s32[1]{0:T(128)} %bitcast.1.refs_0_, s32[1]{0:T(128)} %bitcast.2.refs_1_, s32[4,34]{1,0:T(4,128)} %bitcast.25, f32[4,34]{1,0:T(4,128)} %bitcast.28, bf16[34,6144]{1,0:T(8,128)(2,1)} %refs_4_.1), custom_call_target="tpu_custom_call" | custom-call | tf_op jit(solution)/shard_map/pick/pallas_call | solution.py:118
  2.8 18.2 %all-to-all-start = ((bf16[16,64,128]{2,1,0:T(8,128)(2,1)}), bf16[16,64,128]{2,1,0:T(8,128)(2,1)S(1)}, u32[]{:S(2)}, u32[]{:S(2)}) async-start(bf16[16,64,128]{2,1,0:T(8,128)(2,1)} %bitcast.27), calls=%async_computation | async-start | bytes 524288 | tf_op jit(solution)/shard_map/all_to_all | solution.py:423
  21.0 0.0 copy-start.2
  21.0 1.5 %copy-done.2 = bf16[1,16,10,6144]{3,1,2,0:T(8,128)(2,1)S(1)} copy-done((bf16[1,16,10,6144]{3,1,2,0:T(8,128)(2,1)S(1)}, bf16[1,16,10,6144]{3,1,2,0:T(8,128)(2,1)}, u32[]{:S(2)}) %copy-start.2) | copy-done | bytes 1966104
  22.6 0.0 copy-start.4
  22.6 1.2 copy-done.4
  23.8 0.0 copy-start.5
  23.8 1.2 copy-done.5
  25.1 0.0 copy-start.6
  25.1 1.2 copy-done.6
  26.3 2.4 %forward.1 = (bf16[192,6144]{1,0:T(8,128)(2,1)S(1)}, bf16[96,6144]{1,0:T(8,128)(2,1)S(1)}, f32[160,96]{1,0:T(8,128)S(1)}, f32[160,96]{1,0:T(8,128)S(1)}, f32[160,96]{1,0:T(8,128)S(1)}) custom-call(bf16[160,6144]{1,0:T(8,128)(2,1)S(1)} %bitcast.18, bf16[84,6144]{1,0:T(8,128)(2,1)S(1)} %bitcast.19, bf16[84,6144]{1,0:T(8,128)(2,1)S(1)} %bitcast.20, ...), custom_call_target="tpu_custom_call" | custom-call | flops 330301440 | bytes 10125312 | tf_op jit(solution)/shard_map/forward/pallas_call | solution.py:210
  28.7 0.0 copy-start
  28.7 1.4 %copy-done = bf16[192,6144]{1,0:T(8,128)(2,1)} copy-done((bf16[192,6144]{1,0:T(8,128)(2,1)}, bf16[192,6144]{1,0:T(8,128)(2,1)S(1)}, u32[]{:S(2)}) %copy-start) | copy-done | bytes 2359320
  30.2 2.6 %all-to-all-done = bf16[16,64,128]{2,1,0:T(8,128)(2,1)S(1)} async-done(((bf16[16,64,128]{2,1,0:T(8,128)(2,1)}), bf16[16,64,128]{2,1,0:T(8,128)(2,1)S(1)}, u32[]{:S(2)}, u32[]{:S(2)}) %all-to-all-start) | async-done | bytes 262176 | tf_op jit(solution)/shard_map/all_to_all | solution.py:423
  32.7 0.4 spread.1
  33.1 0.0 copy-start.3
  33.2 1.3 copy-done.3
  34.4 7.3 %all-to-all-start.1 = ((bf16[8,960,128]{2,1,0:T(8,128)(2,1)}), bf16[8,960,128]{2,1,0:T(8,128)(2,1)S(1)}, u32[]{:S(2)}, u32[]{:S(2)}) async-start(bf16[8,960,128]{2,1,0:T(8,128)(2,1)} %copy-done.3), calls=%async_computation.1 | async-start | bytes 3932160 | tf_op jit(solution)/shard_map/all_to_all | solution.py:434
  41.7 27.7 %all-to-all-done.1.refs_1_ = bf16[8,960,128]{2,1,0:T(8,128)(2,1)S(1)} async-done(((bf16[8,960,128]{2,1,0:T(8,128)(2,1)}), bf16[8,960,128]{2,1,0:T(8,128)(2,1)S(1)}, u32[]{:S(2)}, u32[]{:S(2)}) %all-to-all-start.1) | async-done | bytes 1966112 | tf_op jit(solution)/shard_map/all_to_all | solution.py:434
  69.4 0.0 copy-start.1
  69.4 1.7 %copy-done.1 = bf16[192,6144]{1,0:T(8,128)(2,1)S(1)} copy-done((bf16[192,6144]{1,0:T(8,128)(2,1)S(1)}, bf16[192,6144]{1,0:T(8,128)(2,1)}, u32[]{:S(2)}) %copy-start.1) | copy-done | bytes 2359320
  71.1 2.7 %slot_grads.1 = bf16[8,976,128]{2,1,0:T(8,128)(2,1)S(1)} custom-call(s32[1]{0:T(128)} %bitcast.4.refs_0_, bf16[8,960,128]{2,1,0:T(8,128)(2,1)S(1)} %all-to-all-done.1.refs_1_, bf16[96,6144]{1,0:T(8,128)(2,1)S(1)} %get-tuple-element.17.refs_2_, f32[160,96]{1,0:T(8,128)S(1)} %get-tuple-element.15.refs_1_.refs_3_, f32[160,96]{1,0:T(8,128)S(1)} %get-tuple-element.18.refs_4_, ...), custom_call_target="tpu_custom_call" | custom-call | tf_op jit(solution)/shard_map/slot_grads/pallas_call | solution.py:322
  73.8 30.4 %all_to_all.25.recv = bf16[8,976,128]{2,1,0:T(8,128)(2,1)S(1)} all-to-all(bf16[8,976,128]{2,1,0:T(8,128)(2,1)S(1)} %slot_grads.1), channel_id=1, replica_groups={{0,16,32,48,64,80,96,112},{128,144,160,176,192,208,224,240},{256,272,28..., dimensions={0} | all-to-all | bytes 3997696 | tf_op jit(solution)/shard_map/all_to_all | solution.py:434
  104.2 0.0 copy-start.7
  104.2 0.0 copy-start.8
  104.2 0.3 first_sum.1
  104.5 16.7 %all_to_all.26.refs_0_ = bf16[8,176,128]{2,1,0:T(8,128)(2,1)S(1)} all-to-all(bf16[8,176,128]{2,1,0:T(8,128)(2,1)S(1)} %first_sum.1), channel_id=1, replica_groups={{0,128,256,384,512,640,768,896},{16,144,272,400,528,656,784,912},{32,16..., dimensions={0} | all-to-all | bytes 720896 | tf_op jit(solution)/shard_map/all_to_all | solution.py:434
  121.2 0.5 second_sum.1
  121.6 16.7 %all_to_all.27 = bf16[16,16,128]{2,1,0:T(8,128)(2,1)S(1)} all-to-all(bf16[16,16,128]{2,1,0:T(8,128)(2,1)S(1)} %bitcast.24), channel_id=1, replica_groups=mesh['y'=8,'x'=8,'expert'=16] {'expert'}, dimensions={0} | all-to-all | bytes 131072 | tf_op jit(solution)/shard_map/all_to_all | solution.py:423
  138.3 0.0 copy-done.7
  138.3 0.0 copy-done.8
  138.3 0.9 combine.1
Async XLA Ops:
  2.8 29.9 %all-to-all-start = ((bf16[16,64,128]{2,1,0:T(8,128)(2,1)}), bf16[16,64,128]{2,1,0:T(8,128)(2,1)S(1)}, u32[]{:S(2)}, u32[]{:S(2)}) async-start(bf16[16,64,128]{2,1,0:T(8,128)(2,1)} %bitcast.27), calls=%async_computation | async-start | bytes 524288 | tf_op jit(solution)/shard_map/all_to_all | solution.py:423
  21.0 1.5 %copy-start.2 = (bf16[1,16,10,6144]{3,1,2,0:T(8,128)(2,1)S(1)}, bf16[1,16,10,6144]{3,1,2,0:T(8,128)(2,1)}, u32[]{:S(2)}) copy-start(bf16[1,16,10,6144]{3,1,2,0:T(8,128)(2,1)} %param.10) | copy-start | bytes 5898244
  22.6 1.2 copy-start.4
  23.8 1.2 copy-start.5
  25.1 1.2 copy-start.6
  28.7 1.4 %copy-start = (bf16[192,6144]{1,0:T(8,128)(2,1)}, bf16[192,6144]{1,0:T(8,128)(2,1)S(1)}, u32[]{:S(2)}) copy-start(bf16[192,6144]{1,0:T(8,128)(2,1)S(1)} %get-tuple-element.21.refs_7_) | copy-start | bytes 7077892
  33.1 1.3 copy-start.3
  34.4 35.0 %all-to-all-start.1 = ((bf16[8,960,128]{2,1,0:T(8,128)(2,1)}), bf16[8,960,128]{2,1,0:T(8,128)(2,1)S(1)}, u32[]{:S(2)}, u32[]{:S(2)}) async-start(bf16[8,960,128]{2,1,0:T(8,128)(2,1)} %copy-done.3), calls=%async_computation.1 | async-start | bytes 3932160 | tf_op jit(solution)/shard_map/all_to_all | solution.py:434
  69.4 1.7 %copy-start.1 = (bf16[192,6144]{1,0:T(8,128)(2,1)S(1)}, bf16[192,6144]{1,0:T(8,128)(2,1)}, u32[]{:S(2)}) copy-start(bf16[192,6144]{1,0:T(8,128)(2,1)} %copy-done) | copy-start | bytes 7077892
  104.2 34.2 %copy-start.7 = (bf16[160,34]{1,0:T(8,128)(2,1)S(1)}, bf16[160,34]{1,0:T(8,128)(2,1)}, u32[]{:S(2)}) copy-start(bf16[160,34]{1,0:T(8,128)(2,1)} %get-tuple-element.13.picker) | copy-start | bytes 32644
  104.2 34.2 %copy-start.8 = (s32[34,4]{0,1:T(4,128)S(1)}, s32[34,4]{0,1:T(4,128)}, u32[]{:S(2)}) copy-start(s32[34,4]{0,1:T(4,128)} %param.7) | copy-start | bytes 1636

commit v4 on v3

--- a/solution.py
+++ b/solution.py
@@ -50,7 +50,7 @@
 
 
 def pick_kernel(
-    capacity, at_x, at_y, routes_in, probs_in, out_grad, send, picker, routes, probs, grad_x, grad_y, sems
+    capacity, at_x, at_y, _, routes_in, probs_in, out_grad, send, picker, routes, probs, grad_x, grad_y, sems
 ):
     slots, tokens = picker.shape
     experts = slots // capacity
@@ -106,7 +106,7 @@
             send[e * chunk + g * PAD : e * chunk + (g + 1) * PAD, :] = group[e * PAD : (e + 1) * PAD]
 
 
-def pick(at_x, at_y, routes, probs, out_grad, capacity, experts):
+def pick(at_x, at_y, expert, routes, probs, out_grad, capacity, experts):
     tokens, width = out_grad.shape
     part = width // SIDE
     choices = routes.shape[0]
@@ -117,7 +117,7 @@
 
     return pl.pallas_call(
         body,
-        in_specs=[smem(), smem(), hbm(), hbm(), hbm()],
+        in_specs=[smem(), smem(), smem(), hbm(), hbm(), hbm()],
         out_specs=[vmem()] * 2,
         out_shape=[
             jax.ShapeDtypeStruct((experts * chunk, LANES), BF16),
@@ -132,7 +132,7 @@
         ],
         compiler_params=params(63),
         name="pick",
-    )(at_x, at_y, routes, probs, out_grad)
+    )(at_x, at_y, expert, routes, probs, out_grad)
 
 
 def spread_kernel(capacity, recv, after, out, scale):
@@ -160,7 +160,7 @@
 
     return pl.pallas_call(
         body,
-        in_specs=[vmem(), hbm()],
+        in_specs=[vmem(), pl.BlockSpec(memory_space=pl.ANY)],
         out_specs=[vmem(), vmem()],
         out_shape=[
             jax.ShapeDtypeStruct((SIDE, kept, LANES), BF16),
@@ -171,7 +171,7 @@
     )(recv, after)
 
 
-def forward_kernel(inputs, gate_in, up_in, down_in, both, down, activated, by_gate, by_up, pre):
+def forward_kernel(inputs, gate_in, up_in, down_in, both, down, factors, pre):
     contract = (((1,), (1,)), ((), ()))
     hidden, pad = gate_in.shape[0], down.shape[0]
     step = pl.program_id(0)
@@ -194,9 +194,9 @@
         gate, up = pre[:, :pad], pre[:, pad:]
         sigmoid_gate = jax.nn.sigmoid(gate)
         silu_gate = gate * sigmoid_gate
-        activated[...] = (silu_gate * up).astype(BF16).astype(F32)
-        by_gate[...] = up * sigmoid_gate * (1.0 + gate * (1.0 - sigmoid_gate))
-        by_up[...] = silu_gate
+        factors[0] = (silu_gate * up).astype(BF16).astype(F32)
+        factors[1] = up * sigmoid_gate * (1.0 + gate * (1.0 - sigmoid_gate))
+        factors[2] = silu_gate
 
 
 def forward(inputs, w_gate, w_up, w_down):
@@ -205,19 +205,15 @@
     pad = -(-hidden // 32) * 32
     steps = 4
     piece = lambda rows: pl.BlockSpec((rows, width // steps), lambda i: (0, i))
-    factors = pl.BlockSpec((slots, pad), lambda i: (0, 0))
-    shape = jax.ShapeDtypeStruct((slots, pad), F32)
     return pl.pallas_call(
         forward_kernel,
         grid=(steps,),
         in_specs=[piece(slots), piece(hidden), piece(hidden), piece(hidden)],
-        out_specs=[piece(2 * pad), piece(pad), factors, factors, factors],
+        out_specs=[piece(2 * pad), piece(pad), pl.BlockSpec((3, slots, pad), lambda i: (0, 0, 0))],
         out_shape=[
             jax.ShapeDtypeStruct((2 * pad, width), BF16),
             jax.ShapeDtypeStruct((pad, width), BF16),
-            shape,
-            shape,
-            shape,
+            jax.ShapeDtypeStruct((3, slots, pad), F32),
         ],
         scratch_shapes=[pltpu.VMEM((slots, 2 * pad), F32)],
         compiler_params=params(32),
@@ -253,7 +249,7 @@
 
 
 def slot_grads_kernel(
-    capacity, expert, grads, down, activated, by_gate, by_up, scale, both, out, held
+    capacity, expert, grads, down, factors, scale, both, out, held
 ):
     contract = (((1,), (1,)), ((), ()))
     peers, slots, pad = grads.shape[0], scale.shape[0], down.shape[0]
@@ -265,9 +261,9 @@
         back = back + lax.dot_general(
             jnp.concatenate(tiles, axis=1), down[:, columns], contract, preferred_element_type=F32
         )
-    sums = jnp.sum(activated[...] * back, axis=1, keepdims=True)
+    sums = jnp.sum(factors[0] * back, axis=1, keepdims=True)
     scaled = scale[:, :1] * back
-    d_gate, d_up = (scaled * by_gate[...]).astype(BF16), (scaled * by_up[...]).astype(BF16)
+    d_gate, d_up = (scaled * factors[1]).astype(BF16), (scaled * factors[2]).astype(BF16)
     d_both = jnp.concatenate([d_gate, d_up], axis=1)
 
     experts = slots // capacity
@@ -311,7 +307,7 @@
                 out[y, j * slots : (j + 1) * slots, :] = tile_of(y * tiles + j).astype(BF16)
 
 
-def slot_grads(expert, grads, down, activated, by_gate, by_up, scale, both, capacity):
+def slot_grads(expert, grads, down, factors, scale, both, capacity):
     slots = scale.shape[0]
     width = both.shape[1]
     rows = width // SIDE // LANES * slots + PAD
@@ -321,13 +317,13 @@
 
     return pl.pallas_call(
         body,
-        in_specs=[smem()] + [vmem()] * 7,
+        in_specs=[smem()] + [vmem()] * 5,
         out_specs=vmem(),
         out_shape=jax.ShapeDtypeStruct((SIDE, rows, LANES), BF16),
         scratch_shapes=[pltpu.VMEM((slots, width), HELD)],
         compiler_params=params(32),
         name="slot_grads",
-    )(expert, grads, down, activated, by_gate, by_up, scale, both)
+    )(expert, grads, down, factors, scale, both)
 
 
 def total(recv, first, count):
@@ -337,48 +333,73 @@
     return sums
 
 
-def first_sum_kernel(recv, out):
+def fold(slots, share):
+    spare = LANES - share
+    parts = share // spare
+    rest = slots // (parts + 1)
+    return spare, parts, rest
+
+
+def first_sum_kernel(slots, recv, out):
     peers, rows, _ = recv.shape
-    slots = out.shape[1] - PAD
     tiles = (rows - PAD) // slots
     share = tiles * LANES // peers
+    spare, parts, rest = fold(slots, share)
+    kept = slots - rest
     columns = [total(recv, j * slots, slots) for j in range(tiles)]
-    packed = pack_sums(unpack_sums(total(recv, tiles * slots, PAD)))
+    sums = unpack_sums(total(recv, tiles * slots, PAD))
+    half = PAD // 2
+    packed = pack_sums(sums[:half] + pltpu.roll(sums[half:], LANES // 4, axis=1)).astype(F32)
     lane = iota((slots, LANES), 1)
     for peer in range(peers):
         made = None
         for _, low, high, values in cut(lambda tile: columns[tile], peer * share, share, 0):
             made = values if made is None else jnp.where((lane >= low) & (lane < high), values, made)
-        out[peer, :slots, :] = made.astype(BF16)
-        out[peer, slots:, :] = packed
-
-
-def first_sum(recv, slots):
-    return pl.pallas_call(
-        first_sum_kernel,
+        last = [pltpu.roll(made[kept:], share - q * spare, axis=1) for q in range(parts)]
+        grads = jnp.where(lane[:kept] < share, made[:kept], jnp.concatenate(last, axis=0))
+        out[peer] = jnp.concatenate([grads, packed], axis=0).astype(BF16)
+
+
+def first_sum(recv, slots, share):
+    kept = slots - fold(slots, share)[2]
+
+    def body(*refs):
+        first_sum_kernel(slots, *refs)
+
+    return pl.pallas_call(
+        body,
         in_specs=[vmem()],
         out_specs=vmem(),
-        out_shape=jax.ShapeDtypeStruct((SIDE, slots + PAD, LANES), BF16),
+        out_shape=jax.ShapeDtypeStruct((SIDE, kept + PAD // 2, LANES), BF16),
         compiler_params=params(32),
         name="first_sum",
     )(recv)
 
 
-def second_sum_kernel(share, recv, out):
-    slots, rows = recv.shape[1] - PAD, out.shape[0]
+def second_sum_kernel(slots, share, recv, out):
+    rows = out.shape[0]
     experts = rows // PAD
-    grads = total(recv, 0, slots)
-    probs = unpack_sums(total(recv, slots, PAD)).astype(BF16)
-    line = dot(one_hot(iota((slots, PAD), 0) // experts == iota((slots, PAD), 1)), probs)
+    spare, parts, rest = fold(slots, share)
+    kept = slots - rest
+    sums = total(recv, 0, recv.shape[1])
+    side = iota((rest, LANES), 1)
+    last = jnp.zeros((rest, LANES), F32)
+    for q in range(parts):
+        piece = pltpu.roll(sums[q * rest : (q + 1) * rest], (q + 1) * spare, axis=1)
+        last = jnp.where((side >= q * spare) & (side < (q + 1) * spare), piece, last)
+    grads = jnp.concatenate([sums[:kept], last], axis=0)
+    probs = unpack_sums(sums[kept:])
+    probs = jnp.concatenate([probs, pltpu.roll(probs, LANES - LANES // 4, axis=1)], axis=0)
+    line = dot(one_hot(iota((slots, PAD), 0) // experts == iota((slots, PAD), 1)), probs.astype(BF16))
     lane, row = iota((slots, LANES), 1), iota((slots, LANES), 0)
     column = jnp.sum(jnp.where(lane == row % experts, line, 0.0), axis=1, keepdims=True)
     values = jnp.where(lane < share, grads, jnp.where(lane == share, column, 0.0)).astype(BF16)
     out[...] = swap(jnp.concatenate([values, jnp.zeros((rows - slots, LANES), BF16)], axis=0))
 
 
-def second_sum(recv, share, experts):
+def second_sum(recv, slots, share, experts):
     def body(*refs):
-        second_sum_kernel(share, *refs)
+        second_sum_kernel(slots, share, *refs)
 
     return pl.pallas_call(
         body,
@@ -448,16 +469,16 @@
         lax.axis_index(axis).astype(jnp.int32).reshape(1) for axis in ("x", "y", "expert")
     )
 
-    send, picker = pick(at_x, at_y, routes, probs, out_grad, capacity, experts)
+    send, picker = pick(at_x, at_y, expert, routes, probs, out_grad, capacity, experts)
     recv = exchange(send.reshape(experts, -1, LANES)).reshape(-1, LANES)
     inputs = saved_inputs[0].transpose(1, 0, 2).reshape(slots, width)
-    both, down, activated, by_gate, by_up = forward(inputs, w_gate[0], w_up[0], w_down[0])
-
-    shards, scale = spread(recv, activated, width // SIDE, capacity)
+    both, down, factors = forward(inputs, w_gate[0], w_up[0], w_down[0])
+
+    shards, scale = spread(recv, both, width // SIDE, capacity)
     grads = exchange_in_plane(shards, True)
-    parts = slot_grads(expert, grads, down, activated, by_gate, by_up, scale, both, capacity)
-    first = first_sum(exchange_in_plane(parts, True), slots)
-    back = second_sum(exchange_in_plane(first, False), share, experts)
+    parts = slot_grads(expert, grads, down, factors, scale, both, capacity)
+    first = first_sum(exchange_in_plane(parts, True), slots, share)
+    back = second_sum(exchange_in_plane(first, False), slots, share, experts)
     got = exchange(back.reshape(experts, PAD, LANES)).reshape(experts * PAD, LANES)
     in_grad, prob_grad = combine(routes, picker, got, share)
     return in_grad, prob_grad.T

time: 140 us -> 136 us (0.971)
  blocking collectives: 63.7 us -> 96.6 us
  waiting for transfers between devices: 30.3 us -> 3.45 us
  starting transfers between devices: 25.5 us -> 18.2 us
  local copies, waits for them, and re-layouts: 9.61 us -> 5.94 us
    all_to_all x2 -> x3, blocking collectives: 47 us -> 80.8 us  [exchange_in_plane(): lax.all_to_all(values, ('y', 'x', 'expert'), split_axis=0, concat_axis=0,...]
    all_to_all x1 -> x0, waiting for transfers between devices: 27.7 us -> none  [exchange_in_plane(): lax.all_to_all(values, ('y', 'x', 'expert'), split_axis=0, concat_axis=0,...]
    all_to_all x1 -> x0, starting transfers between devices: 7.27 us -> none  [exchange_in_plane(): lax.all_to_all(values, ('y', 'x', 'expert'), split_axis=0, concat_axis=0,...]
    unnamed x18 -> x16, local copies, waits for them, and re-layouts: 9.61 us -> 5.94 us
  transfers between devices with their start and end apart: 2 -> 1, of which waited for: 2 -> 1; matrix products, arithmetic and copies ran while one was open for 0% -> 0% of each run, Pallas kernels for 2% -> 2%
where the time goes in v4:
time: 136 us
  blocking collectives  96.6 us (71%)
  starting transfers between devices  18.2 us (13%)
  Pallas kernels  10.7 us (8%)
  local copies, waits for them, and re-layouts  5.94 us (4%)
  waiting for transfers between devices  3.45 us (3%)
    all_to_all x3, blocking collectives, exchange_in_plane(): lax.all_to_all(values, ('y', 'x', 'expert'), split_axis=0, concat_axis=0,...  80.8 us
    all_to_all x1, starting transfers between devices, exchange(): lax.all_to_all(values, 'expert', split_axis=0, concat_axis=0, tiled=True)  18.2 us
    all_to_all x1, blocking collectives, exchange(): lax.all_to_all(values, 'expert', split_axis=0, concat_axis=0, tiled=True)  15.9 us
    unnamed x16, local copies, waits for them, and re-layouts  5.94 us
    all_to_all x1, waiting for transfers between devices, exchange(): lax.all_to_all(values, 'expert', split_axis=0, concat_axis=0, tiled=True)  3.45 us
  transfers between devices with their start and end apart: 1, of which 1 were waited for; matrix products, arithmetic and copies ran while one was open for 0% of the time, Pallas kernels for 2%

profile of v4, /device:TPU:1, one launch (start us, length us, event | category | flops | bytes accessed | tf_op | source)
XLA Modules:
  0.0 135.7 jit_solution(16344894790934067052)
XLA Ops:
  0.6 2.2 %pick.1 = (bf16[1024,128]{1,0:T(8,128)(2,1)}, bf16[160,34]{1,0:T(8,128)(2,1)}) custom-call(s32[1]{0:T(128)} %bitcast.1.refs_0_, s32[1]{0:T(128)} %bitcast.2.refs_1_, s32[1]{0:T(128)} %bitcast.3.refs_2_.refs_0_, s32[4,34]{1,0:T(4,128)} %bitcast.24, f32[4,34]{1,0:T(4,128)} %bitcast.27, bf16[34,6144]{1,0:T(8,128)(2,1)} %refs_5_.1), custom_call_target="tpu_custom_call" | custom-call | tf_op jit(solution)/shard_map/pick/pallas_call | solution.py:118
  2.8 18.2 %all-to-all-start = ((bf16[16,64,128]{2,1,0:T(8,128)(2,1)}), bf16[16,64,128]{2,1,0:T(8,128)(2,1)}, u32[]{:S(2)}, u32[]{:S(2)}) async-start(bf16[16,64,128]{2,1,0:T(8,128)(2,1)} %bitcast.26), calls=%async_computation | async-start | bytes 524288 | tf_op jit(solution)/shard_map/all_to_all | solution.py:444
  21.0 0.0 copy-start
  21.0 1.5 %copy-done = bf16[1,16,10,6144]{3,1,2,0:T(8,128)(2,1)S(1)} copy-done((bf16[1,16,10,6144]{3,1,2,0:T(8,128)(2,1)S(1)}, bf16[1,16,10,6144]{3,1,2,0:T(8,128)(2,1)}, u32[]{:S(2)}) %copy-start) | copy-done | bytes 1966104
  22.6 0.0 copy-start.1
  22.6 1.2 copy-done.1
  23.8 0.0 copy-start.2
  23.8 1.2 copy-done.2
  25.0 0.0 copy-start.3
  25.0 1.2 copy-done.3
  26.3 2.4 %forward.1 = (bf16[192,6144]{1,0:T(8,128)(2,1)S(1)}, bf16[96,6144]{1,0:T(8,128)(2,1)S(1)}, f32[3,160,96]{2,1,0:T(8,128)S(1)}) custom-call(bf16[160,6144]{1,0:T(8,128)(2,1)S(1)} %bitcast.18, bf16[84,6144]{1,0:T(8,128)(2,1)S(1)} %bitcast.19, bf16[84,6144]{1,0:T(8,128)(2,1)S(1)} %bitcast.20, bf16[84,6144]{1,0:T(8,128)(2,1)S(1)} %bitcast.21), custom_call_target="tpu_custom_call" | custom-call | flops 330301440 | bytes 10125312 | tf_op jit(solution)/shard_map/forward/pallas_call | solution.py:208
  28.7 0.0 copy-start.4
  28.7 0.7 copy-done.4
  29.4 3.4 %all-to-all-done = bf16[16,64,128]{2,1,0:T(8,128)(2,1)} async-done(((bf16[16,64,128]{2,1,0:T(8,128)(2,1)}), bf16[16,64,128]{2,1,0:T(8,128)(2,1)}, u32[]{:S(2)}, u32[]{:S(2)}) %all-to-all-start) | async-done | bytes 262176 | tf_op jit(solution)/shard_map/all_to_all | solution.py:444
  32.8 1.3 spread.1
  34.2 0.0 copy-start.5
  34.2 34.8 %all_to_all.25.refs_1_ = bf16[8,960,128]{2,1,0:T(8,128)(2,1)S(1)} all-to-all(bf16[8,960,128]{2,1,0:T(8,128)(2,1)S(1)} %get-tuple-element.14), channel_id=1, replica_groups={{0,16,32,48,64,80,96,112},{128,144,160,176,192,208,224,240},{256,272,28..., dimensions={0} | all-to-all | bytes 3932160 | tf_op jit(solution)/shard_map/all_to_all | solution.py:455
  69.0 0.0 copy-done.5
  69.0 2.7 %slot_grads.1 = bf16[8,976,128]{2,1,0:T(8,128)(2,1)S(1)} custom-call(s32[1]{0:T(128)} %bitcast.3.refs_2_.refs_0_, bf16[8,960,128]{2,1,0:T(8,128)(2,1)S(1)} %all_to_all.25.refs_1_, bf16[96,6144]{1,0:T(8,128)(2,1)S(1)} %get-tuple-element.15.refs_2_, f32[3,160,96]{2,1,0:T(8,128)S(1)} %copy-done.5, f32[160,128]{1,0:T(8,128)S(1)} %get-tuple-element.17.refs_4_, ...), custom_call_target="tpu_custom_call" | custom-call | tf_op jit(solution)/shard_map/slot_grads/pallas_call | solution.py:318
  71.7 30.4 %all_to_all.26.refs_0_ = bf16[8,976,128]{2,1,0:T(8,128)(2,1)S(1)} all-to-all(bf16[8,976,128]{2,1,0:T(8,128)(2,1)S(1)} %slot_grads.1), channel_id=1, replica_groups={{0,16,32,48,64,80,96,112},{128,144,160,176,192,208,224,240},{256,272,28..., dimensions={0} | all-to-all | bytes 3997696 | tf_op jit(solution)/shard_map/all_to_all | solution.py:455
  102.1 0.0 copy-start.6
  102.1 0.0 copy-start.7
  102.1 0.7 first_sum.1
  102.8 15.6 %all_to_all.27.refs_0_ = bf16[8,128,128]{2,1,0:T(8,128)(2,1)S(1)} all-to-all(bf16[8,128,128]{2,1,0:T(8,128)(2,1)S(1)} %first_sum.1), channel_id=1, replica_groups={{0,128,256,384,512,640,768,896},{16,144,272,400,528,656,784,912},{32,16..., dimensions={0} | all-to-all | bytes 524288 | tf_op jit(solution)/shard_map/all_to_all | solution.py:455
  118.4 0.5 second_sum.1
  118.9 15.9 %all_to_all.28 = bf16[16,16,128]{2,1,0:T(8,128)(2,1)S(1)} all-to-all(bf16[16,16,128]{2,1,0:T(8,128)(2,1)S(1)} %bitcast.22), channel_id=1, replica_groups=mesh['y'=8,'x'=8,'expert'=16] {'expert'}, dimensions={0} | all-to-all | bytes 131072 | tf_op jit(solution)/shard_map/all_to_all | solution.py:444
  134.8 0.0 copy-done.6
  134.8 0.0 copy-done.7
  134.8 0.9 combine.1
Async XLA Ops:
  2.8 30.0 %all-to-all-start = ((bf16[16,64,128]{2,1,0:T(8,128)(2,1)}), bf16[16,64,128]{2,1,0:T(8,128)(2,1)}, u32[]{:S(2)}, u32[]{:S(2)}) async-start(bf16[16,64,128]{2,1,0:T(8,128)(2,1)} %bitcast.26), calls=%async_computation | async-start | bytes 524288 | tf_op jit(solution)/shard_map/all_to_all | solution.py:444
  21.0 1.5 %copy-start = (bf16[1,16,10,6144]{3,1,2,0:T(8,128)(2,1)S(1)}, bf16[1,16,10,6144]{3,1,2,0:T(8,128)(2,1)}, u32[]{:S(2)}) copy-start(bf16[1,16,10,6144]{3,1,2,0:T(8,128)(2,1)} %param.10) | copy-start | bytes 5898244
  22.6 1.2 copy-start.1
  23.8 1.2 copy-start.2
  25.0 1.2 copy-start.3
  28.7 0.7 copy-start.4
  34.2 34.8 %copy-start.5 = (f32[3,160,96]{2,1,0:T(8,128)S(1)}, f32[3,160,96]{2,1,0:T(8,128)}, u32[]{:S(2)}) copy-start(f32[3,160,96]{2,1,0:T(8,128)} %copy-done.4) | copy-start | bytes 552964
  102.1 32.7 %copy-start.6 = (bf16[160,34]{1,0:T(8,128)(2,1)S(1)}, bf16[160,34]{1,0:T(8,128)(2,1)}, u32[]{:S(2)}) copy-start(bf16[160,34]{1,0:T(8,128)(2,1)} %get-tuple-element.11.picker) | copy-start | bytes 32644
  102.1 32.7 %copy-start.7 = (s32[34,4]{0,1:T(4,128)S(1)}, s32[34,4]{0,1:T(4,128)}, u32[]{:S(2)}) copy-start(s32[34,4]{0,1:T(4,128)} %param.7) | copy-start | bytes 1636

commit v5 on v4

--- a/solution.py
+++ b/solution.py
@@ -171,27 +171,26 @@
     )(recv, after)
 
 
-def forward_kernel(inputs, gate_in, up_in, down_in, both, down, factors, pre):
+def forward_kernel(inputs, gate_in, up_in, factors, gate_pre, up_pre):
     contract = (((1,), (1,)), ((), ()))
-    hidden, pad = gate_in.shape[0], down.shape[0]
     step = pl.program_id(0)
-    zeros = jnp.zeros((pad - hidden, gate_in.shape[1]), BF16)
-    weights = jnp.concatenate([gate_in[...], zeros, up_in[...], zeros], axis=0)
-    both[...] = weights
-    down[...] = jnp.concatenate([down_in[...], zeros], axis=0)
-    part = lax.dot_general(inputs[...], weights, contract, preferred_element_type=F32)
+    x = inputs[...]
+    gate_part = lax.dot_general(x, gate_in[...], contract, preferred_element_type=F32)
+    up_part = lax.dot_general(x, up_in[...], contract, preferred_element_type=F32)
 
     @pl.when(step == 0)
     def _():
-        pre[...] = part
+        gate_pre[...] = gate_part
+        up_pre[...] = up_part
 
     @pl.when(step > 0)
     def _():
-        pre[...] += part
+        gate_pre[...] += gate_part
+        up_pre[...] += up_part
 
     @pl.when(step == pl.num_programs(0) - 1)
     def _():
-        gate, up = pre[:, :pad], pre[:, pad:]
+        gate, up = gate_pre[...], up_pre[...]
         sigmoid_gate = jax.nn.sigmoid(gate)
         silu_gate = gate * sigmoid_gate
         factors[0] = (silu_gate * up).astype(BF16).astype(F32)
@@ -199,31 +198,26 @@
         factors[2] = silu_gate
 
 
-def forward(inputs, w_gate, w_up, w_down):
+def forward(inputs, w_gate, w_up):
     slots, width = inputs.shape
     hidden = w_gate.shape[0]
-    pad = -(-hidden // 32) * 32
     steps = 4
     piece = lambda rows: pl.BlockSpec((rows, width // steps), lambda i: (0, i))
     return pl.pallas_call(
         forward_kernel,
         grid=(steps,),
-        in_specs=[piece(slots), piece(hidden), piece(hidden), piece(hidden)],
-        out_specs=[piece(2 * pad), piece(pad), pl.BlockSpec((3, slots, pad), lambda i: (0, 0, 0))],
-        out_shape=[
-            jax.ShapeDtypeStruct((2 * pad, width), BF16),
-            jax.ShapeDtypeStruct((pad, width), BF16),
-            jax.ShapeDtypeStruct((3, slots, pad), F32),
-        ],
-        scratch_shapes=[pltpu.VMEM((slots, 2 * pad), F32)],
+        in_specs=[piece(slots), piece(hidden), piece(hidden)],
+        out_specs=pl.BlockSpec((3, slots, hidden), lambda i: (0, 0, 0)),
+        out_shape=jax.ShapeDtypeStruct((3, slots, hidden), F32),
+        scratch_shapes=[pltpu.VMEM((slots, hidden), F32)] * 2,
         compiler_params=params(32),
         cost_estimate=pl.CostEstimate(
             flops=4 * slots * hidden * width,
-            bytes_accessed=4 * width * (slots + 3 * hidden),
+            bytes_accessed=4 * width * (slots + 2 * hidden),
             transcendentals=0,
         ),
         name="forward",
-    )(inputs, w_gate, w_up, w_down)
+    )(inputs, w_gate, w_up)
 
 
 def pack_sums(total):
@@ -249,7 +243,7 @@
 
 
 def slot_grads_kernel(
-    capacity, expert, grads, down, factors, scale, both, out, held
+    capacity, expert, grads, down, factors, scale, w_gate, w_up, out, held
 ):
     contract = (((1,), (1,)), ((), ()))
     peers, slots, pad = grads.shape[0], scale.shape[0], down.shape[0]
@@ -264,7 +258,6 @@
     sums = jnp.sum(factors[0] * back, axis=1, keepdims=True)
     scaled = scale[:, :1] * back
     d_gate, d_up = (scaled * factors[1]).astype(BF16), (scaled * factors[2]).astype(BF16)
-    d_both = jnp.concatenate([d_gate, d_up], axis=1)
 
     experts = slots // capacity
     grid = jnp.where(iota((slots, LANES), 1) % (LANES // 2) == iota((slots, LANES), 0) % experts, sums, 0.0)
@@ -274,12 +267,13 @@
         total = jnp.where(iota((PAD, LANES), 0) == c, line, total)
     packed = pack_sums(total)
 
-    block = both.shape[1] // SIDE
+    block = w_gate.shape[1] // SIDE
     tiles = block // LANES
     share = block // SIDE
     for y in range(SIDE):
         columns = slice(y * block, (y + 1) * block)
-        held[:, columns] = dot(d_both, both[:, columns]).astype(held.dtype)
+        grad = dot(d_gate, w_gate[:, columns]) + dot(d_up, w_up[:, columns])
+        held[:, columns] = grad.astype(held.dtype)
     for peer in range(SIDE):
         out[peer, tiles * slots :, :] = packed
 
@@ -307,9 +301,9 @@
                 out[y, j * slots : (j + 1) * slots, :] = tile_of(y * tiles + j).astype(BF16)
 
 
-def slot_grads(expert, grads, down, factors, scale, both, capacity):
+def slot_grads(expert, grads, down, factors, scale, w_gate, w_up, capacity):
     slots = scale.shape[0]
-    width = both.shape[1]
+    width = w_gate.shape[1]
     rows = width // SIDE // LANES * slots + PAD
 
     def body(*refs):
@@ -317,13 +311,13 @@
 
     return pl.pallas_call(
         body,
-        in_specs=[smem()] + [vmem()] * 5,
+        in_specs=[smem()] + [vmem()] * 6,
         out_specs=vmem(),
         out_shape=jax.ShapeDtypeStruct((SIDE, rows, LANES), BF16),
         scratch_shapes=[pltpu.VMEM((slots, width), HELD)],
         compiler_params=params(32),
         name="slot_grads",
-    )(expert, grads, down, factors, scale, both)
+    )(expert, grads, down, factors, scale, w_gate, w_up)
 
 
 def total(recv, first, count):
@@ -472,11 +466,13 @@
     send, picker = pick(at_x, at_y, expert, routes, probs, out_grad, capacity, experts)
     recv = exchange(send.reshape(experts, -1, LANES)).reshape(-1, LANES)
     inputs = saved_inputs[0].transpose(1, 0, 2).reshape(slots, width)
-    both, down, factors = forward(inputs, w_gate[0], w_up[0], w_down[0])
-
-    shards, scale = spread(recv, both, width // SIDE, capacity)
+    factors = forward(inputs, w_gate[0], w_up[0])
+
+    shards, scale = spread(recv, factors, width // SIDE, capacity)
     grads = exchange_in_plane(shards, True)
-    parts = slot_grads(expert, grads, down, factors, scale, both, capacity)
+    parts = slot_grads(
+        expert, grads, w_down[0], factors, scale, w_gate[0], w_up[0], capacity
+    )
     first = first_sum(exchange_in_plane(parts, True), slots, share)
     back = second_sum(exchange_in_plane(first, False), slots, share, experts)
     got = exchange(back.reshape(experts, PAD, LANES)).reshape(experts * PAD, LANES)

time: 136 us -> 135 us (level)
  waiting for transfers between devices: 3.45 us -> 5.61 us
  local copies, waits for them, and re-layouts: 5.94 us -> 4.04 us
    all_to_all x1, waiting for transfers between devices: 3.45 us -> 5.61 us  [exchange(): lax.all_to_all(values, 'expert', split_axis=0, concat_axis=0, tiled=True)]
    unnamed x16, local copies, waits for them, and re-layouts: 5.94 us -> 4.04 us
where the time goes in v5:
time: 135 us; the launch traced here: 134 us
  blocking collectives  95.9 us (71%)
  starting transfers between devices  18.2 us (13%)
  Pallas kernels  9.88 us (7%)
  waiting for transfers between devices  5.61 us (4%)
  local copies, waits for them, and re-layouts  4.04 us (3%)
    all_to_all x3, blocking collectives, exchange_in_plane(): lax.all_to_all(values, ('y', 'x', 'expert'), split_axis=0, concat_axis=0,...  80.9 us
    all_to_all x1, starting transfers between devices, exchange(): lax.all_to_all(values, 'expert', split_axis=0, concat_axis=0, tiled=True)  18.2 us
    all_to_all x1, blocking collectives, exchange(): lax.all_to_all(values, 'expert', split_axis=0, concat_axis=0, tiled=True)  15 us
    all_to_all x1, waiting for transfers between devices, exchange(): lax.all_to_all(values, 'expert', split_axis=0, concat_axis=0, tiled=True)  5.61 us
    unnamed x16, local copies, waits for them, and re-layouts  4.04 us
    pallas_call x1, Pallas kernels, slot_grads(): pl.pallas_call(body, in_specs=[smem()] + [vmem()] * 6, out_specs=vmem(),...  3.14 us
  transfers between devices with their start and end apart: 1, of which 1 were waited for; matrix products, arithmetic and copies ran while one was open for 0% of the time, Pallas kernels for 2%

profile of v5, /device:TPU:1, one launch (start us, length us, event | category | flops | bytes accessed | tf_op | source)
XLA Modules:
  0.0 134.3 jit_solution(5904216180471854074)
XLA Ops:
  0.6 2.2 %pick.1 = (bf16[1024,128]{1,0:T(8,128)(2,1)}, bf16[160,34]{1,0:T(8,128)(2,1)}) custom-call(s32[1]{0:T(128)} %bitcast.1.refs_0_, s32[1]{0:T(128)} %bitcast.2.refs_1_, s32[1]{0:T(128)} %bitcast.3.refs_2_.refs_0_, s32[4,34]{1,0:T(4,128)} %bitcast.27, f32[4,34]{1,0:T(4,128)} %bitcast.30, bf16[34,6144]{1,0:T(8,128)(2,1)} %refs_5_.1), custom_call_target="tpu_custom_call" | custom-call | tf_op jit(solution)/shard_map/pick/pallas_call | solution.py:118
  2.8 18.2 %all-to-all-start = ((bf16[16,64,128]{2,1,0:T(8,128)(2,1)}), bf16[16,64,128]{2,1,0:T(8,128)(2,1)S(1)}, u32[]{:S(2)}, u32[]{:S(2)}) async-start(bf16[16,64,128]{2,1,0:T(8,128)(2,1)} %bitcast.29), calls=%async_computation | async-start | bytes 524288 | tf_op jit(solution)/shard_map/all_to_all | solution.py:438
  21.0 0.0 copy-start
  21.0 1.2 copy-done
  22.3 0.0 copy-start.2
  22.3 1.2 copy-done.2
  23.5 0.0 copy-start.4
  23.5 1.5 %copy-done.4 = bf16[1,16,10,6144]{3,1,2,0:T(8,128)(2,1)S(1)} copy-done((bf16[1,16,10,6144]{3,1,2,0:T(8,128)(2,1)S(1)}, bf16[1,16,10,6144]{3,1,2,0:T(8,128)(2,1)}, u32[]{:S(2)}) %copy-start.4) | copy-done | bytes 1966104
  25.0 2.1 %forward.1.refs_1_.refs_3_ = f32[3,160,84]{2,1,0:T(8,128)S(1)} custom-call(bf16[160,6144]{1,0:T(8,128)(2,1)S(1)} %bitcast.22, bf16[84,6144]{1,0:T(8,128)(2,1)S(1)} %bitcast.18, bf16[84,6144]{1,0:T(8,128)(2,1)S(1)} %bitcast.20), custom_call_target="tpu_custom_call" | custom-call | flops 330301440 | bytes 8060928 | tf_op jit(solution)/shard_map/forward/pallas_call | solution.py:206
  27.1 5.6 %all-to-all-done = bf16[16,64,128]{2,1,0:T(8,128)(2,1)S(1)} async-done(((bf16[16,64,128]{2,1,0:T(8,128)(2,1)}), bf16[16,64,128]{2,1,0:T(8,128)(2,1)S(1)}, u32[]{:S(2)}, u32[]{:S(2)}) %all-to-all-start) | async-done | bytes 262176 | tf_op jit(solution)/shard_map/all_to_all | solution.py:438
  32.7 0.4 spread.1
  33.1 0.0 copy-start.1
  33.1 0.0 copy-start.3
  33.2 0.0 copy-start.5
  33.2 34.9 %all_to_all.25.refs_1_ = bf16[8,960,128]{2,1,0:T(8,128)(2,1)S(1)} all-to-all(bf16[8,960,128]{2,1,0:T(8,128)(2,1)S(1)} %get-tuple-element.10), channel_id=1, replica_groups={{0,16,32,48,64,80,96,112},{128,144,160,176,192,208,224,240},{256,272,28..., dimensions={0} | all-to-all | bytes 3932160 | tf_op jit(solution)/shard_map/all_to_all | solution.py:449
  68.1 0.0 copy-done.1
  68.1 0.0 copy-done.3
  68.1 0.0 copy-done.5
  68.1 3.1 %slot_grads.1 = bf16[8,976,128]{2,1,0:T(8,128)(2,1)S(1)} custom-call(s32[1]{0:T(128)} %bitcast.3.refs_2_.refs_0_, bf16[8,960,128]{2,1,0:T(8,128)(2,1)S(1)} %all_to_all.25.refs_1_, bf16[84,6144]{1,0:T(8,128)(2,1)S(1)} %bitcast.23, f32[3,160,84]{2,1,0:T(8,128)S(1)} %forward.1.refs_1_.refs_3_, f32[160,128]{1,0:T(8,128)S(1)} %get-tuple-element.11.refs_4_, ...), custom_call_target="tpu_custom_call" | custom-call | tf_op jit(solution)/shard_map/slot_grads/pallas_call | solution.py:312
  71.2 30.4 %all_to_all.26.refs_0_ = bf16[8,976,128]{2,1,0:T(8,128)(2,1)S(1)} all-to-all(bf16[8,976,128]{2,1,0:T(8,128)(2,1)S(1)} %slot_grads.1), channel_id=1, replica_groups={{0,16,32,48,64,80,96,112},{128,144,160,176,192,208,224,240},{256,272,28..., dimensions={0} | all-to-all | bytes 3997696 | tf_op jit(solution)/shard_map/all_to_all | solution.py:449
  101.6 0.0 copy-start.6
  101.6 0.0 copy-start.7
  101.6 0.7 first_sum.1
  102.3 15.6 %all_to_all.27.refs_0_ = bf16[8,128,128]{2,1,0:T(8,128)(2,1)S(1)} all-to-all(bf16[8,128,128]{2,1,0:T(8,128)(2,1)S(1)} %first_sum.1), channel_id=1, replica_groups={{0,128,256,384,512,640,768,896},{16,144,272,400,528,656,784,912},{32,16..., dimensions={0} | all-to-all | bytes 524288 | tf_op jit(solution)/shard_map/all_to_all | solution.py:449
  117.9 0.5 second_sum.1
  118.5 15.0 %all_to_all.28 = bf16[16,16,128]{2,1,0:T(8,128)(2,1)S(1)} all-to-all(bf16[16,16,128]{2,1,0:T(8,128)(2,1)S(1)} %bitcast.25), channel_id=1, replica_groups=mesh['y'=8,'x'=8,'expert'=16] {'expert'}, dimensions={0} | all-to-all | bytes 131072 | tf_op jit(solution)/shard_map/all_to_all | solution.py:438
  133.4 0.0 copy-done.6
  133.4 0.0 copy-done.7
  133.4 0.9 combine.1
Async XLA Ops:
  2.8 29.9 %all-to-all-start = ((bf16[16,64,128]{2,1,0:T(8,128)(2,1)}), bf16[16,64,128]{2,1,0:T(8,128)(2,1)S(1)}, u32[]{:S(2)}, u32[]{:S(2)}) async-start(bf16[16,64,128]{2,1,0:T(8,128)(2,1)} %bitcast.29), calls=%async_computation | async-start | bytes 524288 | tf_op jit(solution)/shard_map/all_to_all | solution.py:438
  21.0 1.2 copy-start
  22.3 1.2 copy-start.2
  23.5 1.5 %copy-start.4 = (bf16[1,16,10,6144]{3,1,2,0:T(8,128)(2,1)S(1)}, bf16[1,16,10,6144]{3,1,2,0:T(8,128)(2,1)}, u32[]{:S(2)}) copy-start(bf16[1,16,10,6144]{3,1,2,0:T(8,128)(2,1)} %param.10) | copy-start | bytes 5898244
  33.1 35.0 %copy-start.1 = (bf16[1,84,6144]{2,1,0:T(8,128)(2,1)S(1)}, bf16[1,84,6144]{2,1,0:T(8,128)(2,1)}, u32[]{:S(2)}) copy-start(bf16[1,84,6144]{2,1,0:T(8,128)(2,1)} %param.11) | copy-start | bytes 3096580
  33.1 35.0 %copy-start.3 = (bf16[1,84,6144]{2,1,0:T(8,128)(2,1)S(1)}, bf16[1,84,6144]{2,1,0:T(8,128)(2,1)}, u32[]{:S(2)}) copy-start(bf16[1,84,6144]{2,1,0:T(8,128)(2,1)} %param.12) | copy-start | bytes 3096580
  33.2 34.9 %copy-start.5 = (bf16[1,84,6144]{2,1,0:T(8,128)(2,1)S(1)}, bf16[1,84,6144]{2,1,0:T(8,128)(2,1)}, u32[]{:S(2)}) copy-start(bf16[1,84,6144]{2,1,0:T(8,128)(2,1)} %param.13) | copy-start | bytes 3096580
  101.6 31.8 %copy-start.6 = (bf16[160,34]{1,0:T(8,128)(2,1)S(1)}, bf16[160,34]{1,0:T(8,128)(2,1)}, u32[]{:S(2)}) copy-start(bf16[160,34]{1,0:T(8,128)(2,1)} %get-tuple-element.8.picker) | copy-start | bytes 32644
  101.6 31.8 %copy-start.7 = (s32[34,4]{0,1:T(4,128)S(1)}, s32[34,4]{0,1:T(4,128)}, u32[]{:S(2)}) copy-start(s32[34,4]{0,1:T(4,128)} %param.7) | copy-start | bytes 1636

commit v6 on v5

--- a/solution.py
+++ b/solution.py
@@ -135,7 +135,7 @@
     )(at_x, at_y, expert, routes, probs, out_grad)
 
 
-def spread_kernel(capacity, recv, after, out, scale):
+def spread_kernel(capacity, recv, factors, down, out, scale):
     chunk = recv.shape[0] // PAD
     moved = []
     for g in range(chunk // PAD):
@@ -151,7 +151,7 @@
         scale[c * PAD : (c + 1) * PAD, :] = column
 
 
-def spread(recv, after, part, capacity):
+def spread(recv, factors, down, part, capacity):
     slots = PAD * capacity
     kept = part // LANES * slots
 
@@ -160,7 +160,7 @@
 
     return pl.pallas_call(
         body,
-        in_specs=[vmem(), pl.BlockSpec(memory_space=pl.ANY)],
+        in_specs=[vmem()] + [pl.BlockSpec(memory_space=pl.ANY)] * 2,
         out_specs=[vmem(), vmem()],
         out_shape=[
             jax.ShapeDtypeStruct((SIDE, kept, LANES), BF16),
@@ -168,7 +168,7 @@
         ],
         compiler_params=params(32),
         name="spread",
-    )(recv, after)
+    )(recv, factors, down)
 
 
 def forward_kernel(inputs, gate_in, up_in, factors, gate_pre, up_pre):
@@ -245,20 +245,19 @@
 def slot_grads_kernel(
     capacity, expert, grads, down, factors, scale, w_gate, w_up, out, held
 ):
-    contract = (((1,), (1,)), ((), ()))
-    peers, slots, pad = grads.shape[0], scale.shape[0], down.shape[0]
-    part = down.shape[1] // peers
-    back = jnp.zeros((slots, pad), F32)
-    for peer in range(peers):
-        columns = slice(peer * part, (peer + 1) * part)
-        tiles = [grads[peer, j * slots : (j + 1) * slots, :] for j in range(part // LANES)]
-        back = back + lax.dot_general(
-            jnp.concatenate(tiles, axis=1), down[:, columns], contract, preferred_element_type=F32
-        )
+    peers, slots = grads.shape[0], scale.shape[0]
+    part = down.shape[0] // peers
+    tiles = [
+        grads[peer, j * slots : (j + 1) * slots, :]
+        for peer in range(peers)
+        for j in range(part // LANES)
+    ]
+    back = dot(jnp.concatenate(tiles, axis=1), down[...])
     sums = jnp.sum(factors[0] * back, axis=1, keepdims=True)
     scaled = scale[:, :1] * back
     d_gate, d_up = (scaled * factors[1]).astype(BF16), (scaled * factors[2]).astype(BF16)
 
+    d_both = jnp.concatenate([d_gate, d_up], axis=1)
     experts = slots // capacity
     grid = jnp.where(iota((slots, LANES), 1) % (LANES // 2) == iota((slots, LANES), 0) % experts, sums, 0.0)
     rows = [jnp.sum(grid[c * experts : (c + 1) * experts], axis=0, keepdims=True) for c in range(capacity)]
@@ -272,7 +271,7 @@
     share = block // SIDE
     for y in range(SIDE):
         columns = slice(y * block, (y + 1) * block)
-        grad = dot(d_gate, w_gate[:, columns]) + dot(d_up, w_up[:, columns])
+        grad = dot(d_both, jnp.concatenate([w_gate[:, columns], w_up[:, columns]], axis=0))
         held[:, columns] = grad.astype(held.dtype)
     for peer in range(SIDE):
         out[peer, tiles * slots :, :] = packed
@@ -467,11 +466,12 @@
     recv = exchange(send.reshape(experts, -1, LANES)).reshape(-1, LANES)
     inputs = saved_inputs[0].transpose(1, 0, 2).reshape(slots, width)
     factors = forward(inputs, w_gate[0], w_up[0])
-
-    shards, scale = spread(recv, factors, width // SIDE, capacity)
+    down = w_down[0].T
+
+    shards, scale = spread(recv, factors, down, width // SIDE, capacity)
     grads = exchange_in_plane(shards, True)
     parts = slot_grads(
-        expert, grads, w_down[0], factors, scale, w_gate[0], w_up[0], capacity
+        expert, grads, down, factors, scale, w_gate[0], w_up[0], capacity
     )
     first = first_sum(exchange_in_plane(parts, True), slots, share)
     back = second_sum(exchange_in_plane(first, False), slots, share, experts)

time: 135 us -> 133 us (0.985)
  Pallas kernels: 9.88 us -> 8.49 us
    pallas_call x1, Pallas kernels: 3.14 us -> 1.73 us  [slot_grads(): pl.pallas_call(body, in_specs=[smem()] + [vmem()] * 6, out_specs=vmem(),...]
    unnamed x16 -> x13, local copies, waits for them, and re-layouts: 4.04 us -> 4.63 us
  transfers between devices with their start and end apart: 1 -> 1, of which waited for: 1 -> 1; matrix products, arithmetic and copies ran while one was open for 0% -> 1% of each run, Pallas kernels for 2% -> 2%
where the time goes in v6:
time: 133 us
  blocking collectives  95.7 us (72%)
  starting transfers between devices  18.3 us (14%)
  Pallas kernels  8.49 us (6%)
  waiting for transfers between devices  4.99 us (4%)
  local copies, waits for them, and re-layouts  4.63 us (3%)
    all_to_all x3, blocking collectives, exchange_in_plane(): lax.all_to_all(values, ('y', 'x', 'expert'), split_axis=0, concat_axis=0,...  80.8 us
    all_to_all x1, starting transfers between devices, exchange(): lax.all_to_all(values, 'expert', split_axis=0, concat_axis=0, tiled=True)  18.3 us
    all_to_all x1, blocking collectives, exchange(): lax.all_to_all(values, 'expert', split_axis=0, concat_axis=0, tiled=True)  15 us
    all_to_all x1, waiting for transfers between devices, exchange(): lax.all_to_all(values, 'expert', split_axis=0, concat_axis=0, tiled=True)  4.99 us
    unnamed x13, local copies, waits for them, and re-layouts  4.63 us
  transfers between devices with their start and end apart: 1, of which 1 were waited for; matrix products, arithmetic and copies ran while one was open for 1% of the time, Pallas kernels for 2%

profile of v6, /device:TPU:1, one launch (start us, length us, event | category | flops | bytes accessed | tf_op | source)
XLA Modules:
  0.0 132.9 jit_solution(13423846284777680937)
XLA Ops:
  0.6 2.2 %pick.1 = (bf16[1024,128]{1,0:T(8,128)(2,1)}, bf16[160,34]{1,0:T(8,128)(2,1)}) custom-call(s32[1]{0:T(128)} %bitcast.1.refs_0_, s32[1]{0:T(128)} %bitcast.2.refs_1_, s32[1]{0:T(128)} %bitcast.3.refs_2_.refs_0_, s32[4,34]{1,0:T(4,128)} %bitcast.30, f32[4,34]{1,0:T(4,128)} %bitcast.33, bf16[34,6144]{1,0:T(8,128)(2,1)} %refs_5_.1), custom_call_target="tpu_custom_call" | custom-call | tf_op jit(solution)/shard_map/pick/pallas_call | solution.py:118
  2.8 0.0 copy-start
  2.8 18.3 %all-to-all-start = ((bf16[16,64,128]{2,1,0:T(8,128)(2,1)}), bf16[16,64,128]{2,1,0:T(8,128)(2,1)S(1)}, u32[]{:S(2)}, u32[]{:S(2)}) async-start(bf16[16,64,128]{2,1,0:T(8,128)(2,1)} %bitcast.32), calls=%async_computation | async-start | bytes 524288 | tf_op jit(solution)/shard_map/all_to_all | solution.py:437
  21.2 1.8 %copy.9 = bf16[1,84,6144]{1,2,0:T(8,128)(2,1)S(1)} copy(bf16[1,84,6144]{2,1,0:T(8,128)(2,1)} %param.13) | data formatting | bytes 2064384 | tf_op args[6]
  23.0 0.0 copy-done
  23.0 0.0 copy-start.1
  23.0 1.2 copy-done.1
  24.3 0.0 copy-start.3
  24.3 1.5 %copy-done.3 = bf16[1,16,10,6144]{3,1,2,0:T(8,128)(2,1)S(1)} copy-done((bf16[1,16,10,6144]{3,1,2,0:T(8,128)(2,1)S(1)}, bf16[1,16,10,6144]{3,1,2,0:T(8,128)(2,1)}, u32[]{:S(2)}) %copy-start.3) | copy-done | bytes 1966104
  25.8 2.1 %forward.1.refs_1_.refs_3_ = f32[3,160,84]{2,1,0:T(8,128)S(1)} custom-call(bf16[160,6144]{1,0:T(8,128)(2,1)S(1)} %bitcast.26, bf16[84,6144]{1,0:T(8,128)(2,1)S(1)} %bitcast.22, bf16[84,6144]{1,0:T(8,128)(2,1)S(1)} %bitcast.24), custom_call_target="tpu_custom_call" | custom-call | flops 330301440 | bytes 8060928 | tf_op jit(solution)/shard_map/forward/pallas_call | solution.py:206
  27.9 5.0 %all-to-all-done = bf16[16,64,128]{2,1,0:T(8,128)(2,1)S(1)} async-done(((bf16[16,64,128]{2,1,0:T(8,128)(2,1)}), bf16[16,64,128]{2,1,0:T(8,128)(2,1)S(1)}, u32[]{:S(2)}, u32[]{:S(2)}) %all-to-all-start) | async-done | bytes 262176 | tf_op jit(solution)/shard_map/all_to_all | solution.py:437
  32.9 0.4 spread.1
  33.3 0.0 copy-start.2
  33.3 34.8 %all_to_all.25.refs_1_ = bf16[8,960,128]{2,1,0:T(8,128)(2,1)S(1)} all-to-all(bf16[8,960,128]{2,1,0:T(8,128)(2,1)S(1)} %get-tuple-element.10), channel_id=1, replica_groups={{0,16,32,48,64,80,96,112},{128,144,160,176,192,208,224,240},{256,272,28..., dimensions={0} | all-to-all | bytes 3932160 | tf_op jit(solution)/shard_map/all_to_all | solution.py:448
  68.1 0.0 copy-done.2
  68.1 1.7 %slot_grads.1 = bf16[8,976,128]{2,1,0:T(8,128)(2,1)S(1)} custom-call(s32[1]{0:T(128)} %bitcast.3.refs_2_.refs_0_, bf16[8,960,128]{2,1,0:T(8,128)(2,1)S(1)} %all_to_all.25.refs_1_, bf16[6144,84]{1,0:T(8,128)(2,1)S(1)} %bitcast.21, f32[3,160,84]{2,1,0:T(8,128)S(1)} %forward.1.refs_1_.refs_3_, f32[160,128]{1,0:T(8,128)S(1)} %get-tuple-element.11.refs_4_, ...), custom_call_target="tpu_custom_call" | custom-call | tf_op jit(solution)/shard_map/slot_grads/pallas_call | solution.py:311
  69.8 30.4 %all_to_all.26.refs_0_ = bf16[8,976,128]{2,1,0:T(8,128)(2,1)S(1)} all-to-all(bf16[8,976,128]{2,1,0:T(8,128)(2,1)S(1)} %slot_grads.1), channel_id=1, replica_groups={{0,16,32,48,64,80,96,112},{128,144,160,176,192,208,224,240},{256,272,28..., dimensions={0} | all-to-all | bytes 3997696 | tf_op jit(solution)/shard_map/all_to_all | solution.py:448
  100.2 0.0 copy-start.4
  100.2 0.0 copy-start.5
  100.2 0.7 first_sum.1
  100.9 15.6 %all_to_all.27.refs_0_ = bf16[8,128,128]{2,1,0:T(8,128)(2,1)S(1)} all-to-all(bf16[8,128,128]{2,1,0:T(8,128)(2,1)S(1)} %first_sum.1), channel_id=1, replica_groups={{0,128,256,384,512,640,768,896},{16,144,272,400,528,656,784,912},{32,16..., dimensions={0} | all-to-all | bytes 524288 | tf_op jit(solution)/shard_map/all_to_all | solution.py:448
  116.5 0.5 second_sum.1
  117.0 15.0 %all_to_all.28 = bf16[16,16,128]{2,1,0:T(8,128)(2,1)S(1)} all-to-all(bf16[16,16,128]{2,1,0:T(8,128)(2,1)S(1)} %bitcast.28), channel_id=1, replica_groups=mesh['y'=8,'x'=8,'expert'=16] {'expert'}, dimensions={0} | all-to-all | bytes 131072 | tf_op jit(solution)/shard_map/all_to_all | solution.py:437
  132.0 0.0 copy-done.4
  132.0 0.0 copy-done.5
  132.0 0.9 combine.1
Async XLA Ops:
  2.8 20.2 %copy-start = (bf16[1,84,6144]{2,1,0:T(8,128)(2,1)S(1)}, bf16[1,84,6144]{2,1,0:T(8,128)(2,1)}, u32[]{:S(2)}) copy-start(bf16[1,84,6144]{2,1,0:T(8,128)(2,1)} %param.11) | copy-start | bytes 3096580
  2.8 30.1 %all-to-all-start = ((bf16[16,64,128]{2,1,0:T(8,128)(2,1)}), bf16[16,64,128]{2,1,0:T(8,128)(2,1)S(1)}, u32[]{:S(2)}, u32[]{:S(2)}) async-start(bf16[16,64,128]{2,1,0:T(8,128)(2,1)} %bitcast.32), calls=%async_computation | async-start | bytes 524288 | tf_op jit(solution)/shard_map/all_to_all | solution.py:437
  23.0 1.2 copy-start.1
  24.3 1.5 %copy-start.3 = (bf16[1,16,10,6144]{3,1,2,0:T(8,128)(2,1)S(1)}, bf16[1,16,10,6144]{3,1,2,0:T(8,128)(2,1)}, u32[]{:S(2)}) copy-start(bf16[1,16,10,6144]{3,1,2,0:T(8,128)(2,1)} %param.10) | copy-start | bytes 5898244
  33.3 34.8 %copy-start.2 = (bf16[1,84,6144]{2,1,0:T(8,128)(2,1)S(1)}, bf16[1,84,6144]{2,1,0:T(8,128)(2,1)}, u32[]{:S(2)}) copy-start(bf16[1,84,6144]{2,1,0:T(8,128)(2,1)} %param.12) | copy-start | bytes 3096580
  100.2 31.8 %copy-start.4 = (bf16[160,34]{1,0:T(8,128)(2,1)S(1)}, bf16[160,34]{1,0:T(8,128)(2,1)}, u32[]{:S(2)}) copy-start(bf16[160,34]{1,0:T(8,128)(2,1)} %get-tuple-element.8.picker) | copy-start | bytes 32644
  100.2 31.8 %copy-start.5 = (s32[34,4]{0,1:T(4,128)S(1)}, s32[34,4]{0,1:T(4,128)}, u32[]{:S(2)}) copy-start(s32[34,4]{0,1:T(4,128)} %param.7) | copy-start | bytes 1636

commit v7 on v6

--- a/solution.py
+++ b/solution.py
@@ -279,7 +279,7 @@
     def tile_of(tile):
         return held[:, tile * LANES : (tile + 1) * LANES]
 
-    @pl.when(expert[0] % 2 == 0)
+    @pl.when(expert[0] % 2 == 1)
     def _():
         lane = iota((slots, LANES), 1)
         for x in range(SIDE):
@@ -293,7 +293,7 @@
             for j in range(tiles):
                 out[x, j * slots : (j + 1) * slots, :] = made[j].astype(BF16)
 
-    @pl.when(expert[0] % 2 == 1)
+    @pl.when(expert[0] % 2 == 0)
     def _():
         for y in range(SIDE):
             for j in range(tiles):
@@ -473,8 +473,8 @@
     parts = slot_grads(
         expert, grads, down, factors, scale, w_gate[0], w_up[0], capacity
     )
-    first = first_sum(exchange_in_plane(parts, True), slots, share)
-    back = second_sum(exchange_in_plane(first, False), slots, share, experts)
+    first = first_sum(exchange_in_plane(parts, False), slots, share)
+    back = second_sum(exchange_in_plane(first, True), slots, share, experts)
     got = exchange(back.reshape(experts, PAD, LANES)).reshape(experts * PAD, LANES)
     in_grad, prob_grad = combine(routes, picker, got, share)
     return in_grad, prob_grad.T

time: 133 us -> 133 us (level)
  no operation moved by 1% of the time
where the time goes in v7:
time: 133 us; the launch traced here: 132 us
  blocking collectives  94.8 us (71%)
  starting transfers between devices  18.3 us (14%)
  Pallas kernels  8.96 us (7%)
  waiting for transfers between devices  4.99 us (4%)
  local copies, waits for them, and re-layouts  4.63 us (3%)
    all_to_all x3, blocking collectives, exchange_in_plane(): lax.all_to_all(values, ('y', 'x', 'expert'), split_axis=0, concat_axis=0,...  80.8 us
    all_to_all x1, starting transfers between devices, exchange(): lax.all_to_all(values, 'expert', split_axis=0, concat_axis=0, tiled=True)  18.3 us
    all_to_all x1, blocking collectives, exchange(): lax.all_to_all(values, 'expert', split_axis=0, concat_axis=0, tiled=True)  14 us
    all_to_all x1, waiting for transfers between devices, exchange(): lax.all_to_all(values, 'expert', split_axis=0, concat_axis=0, tiled=True)  4.99 us
    unnamed x13, local copies, waits for them, and re-layouts  4.63 us
  transfers between devices with their start and end apart: 1, of which 1 were waited for; matrix products, arithmetic and copies ran while one was open for 1% of the time, Pallas kernels for 2%

profile of v7, /device:TPU:1, one launch (start us, length us, event | category | flops | bytes accessed | tf_op | source)
XLA Modules:
  0.0 132.4 jit_solution(4715530579988482159)
XLA Ops:
  0.6 2.2 %pick.1 = (bf16[1024,128]{1,0:T(8,128)(2,1)}, bf16[160,34]{1,0:T(8,128)(2,1)}) custom-call(s32[1]{0:T(128)} %bitcast.1.refs_0_, s32[1]{0:T(128)} %bitcast.2.refs_1_, s32[1]{0:T(128)} %bitcast.3.refs_2_.refs_0_, s32[4,34]{1,0:T(4,128)} %bitcast.30, f32[4,34]{1,0:T(4,128)} %bitcast.33, bf16[34,6144]{1,0:T(8,128)(2,1)} %refs_5_.1), custom_call_target="tpu_custom_call" | custom-call | tf_op jit(solution)/shard_map/pick/pallas_call | solution.py:118
  2.8 0.0 copy-start
  2.8 18.3 %all-to-all-start = ((bf16[16,64,128]{2,1,0:T(8,128)(2,1)}), bf16[16,64,128]{2,1,0:T(8,128)(2,1)S(1)}, u32[]{:S(2)}, u32[]{:S(2)}) async-start(bf16[16,64,128]{2,1,0:T(8,128)(2,1)} %bitcast.32), calls=%async_computation | async-start | bytes 524288 | tf_op jit(solution)/shard_map/all_to_all | solution.py:437
  21.2 1.8 %copy.9 = bf16[1,84,6144]{1,2,0:T(8,128)(2,1)S(1)} copy(bf16[1,84,6144]{2,1,0:T(8,128)(2,1)} %param.13) | data formatting | bytes 2064384 | tf_op args[6]
  23.0 0.0 copy-done
  23.0 0.0 copy-start.1
  23.0 1.2 copy-done.1
  24.3 0.0 copy-start.3
  24.3 1.5 %copy-done.3 = bf16[1,16,10,6144]{3,1,2,0:T(8,128)(2,1)S(1)} copy-done((bf16[1,16,10,6144]{3,1,2,0:T(8,128)(2,1)S(1)}, bf16[1,16,10,6144]{3,1,2,0:T(8,128)(2,1)}, u32[]{:S(2)}) %copy-start.3) | copy-done | bytes 1966104
  25.8 2.1 %forward.1.refs_1_.refs_3_ = f32[3,160,84]{2,1,0:T(8,128)S(1)} custom-call(bf16[160,6144]{1,0:T(8,128)(2,1)S(1)} %bitcast.26, bf16[84,6144]{1,0:T(8,128)(2,1)S(1)} %bitcast.22, bf16[84,6144]{1,0:T(8,128)(2,1)S(1)} %bitcast.24), custom_call_target="tpu_custom_call" | custom-call | flops 330301440 | bytes 8060928 | tf_op jit(solution)/shard_map/forward/pallas_call | solution.py:206
  27.9 5.0 %all-to-all-done = bf16[16,64,128]{2,1,0:T(8,128)(2,1)S(1)} async-done(((bf16[16,64,128]{2,1,0:T(8,128)(2,1)}), bf16[16,64,128]{2,1,0:T(8,128)(2,1)S(1)}, u32[]{:S(2)}, u32[]{:S(2)}) %all-to-all-start) | async-done | bytes 262176 | tf_op jit(solution)/shard_map/all_to_all | solution.py:437
  32.9 0.4 spread.1
  33.3 0.0 copy-start.2
  33.3 34.8 %all_to_all.25.refs_1_ = bf16[8,960,128]{2,1,0:T(8,128)(2,1)S(1)} all-to-all(bf16[8,960,128]{2,1,0:T(8,128)(2,1)S(1)} %get-tuple-element.10), channel_id=1, replica_groups={{0,16,32,48,64,80,96,112},{128,144,160,176,192,208,224,240},{256,272,28..., dimensions={0} | all-to-all | bytes 3932160 | tf_op jit(solution)/shard_map/all_to_all | solution.py:448
  68.1 0.0 copy-done.2
  68.1 2.2 %slot_grads.1 = bf16[8,976,128]{2,1,0:T(8,128)(2,1)S(1)} custom-call(s32[1]{0:T(128)} %bitcast.3.refs_2_.refs_0_, bf16[8,960,128]{2,1,0:T(8,128)(2,1)S(1)} %all_to_all.25.refs_1_, bf16[6144,84]{1,0:T(8,128)(2,1)S(1)} %bitcast.21, f32[3,160,84]{2,1,0:T(8,128)S(1)} %forward.1.refs_1_.refs_3_, f32[160,128]{1,0:T(8,128)S(1)} %get-tuple-element.11.refs_4_, ...), custom_call_target="tpu_custom_call" | custom-call | tf_op jit(solution)/shard_map/slot_grads/pallas_call | solution.py:311
  70.3 34.2 %all_to_all.26.refs_0_ = bf16[8,976,128]{2,1,0:T(8,128)(2,1)S(1)} all-to-all(bf16[8,976,128]{2,1,0:T(8,128)(2,1)S(1)} %slot_grads.1), channel_id=1, replica_groups={{0,128,256,384,512,640,768,896},{16,144,272,400,528,656,784,912},{32,16..., dimensions={0} | all-to-all | bytes 3997696 | tf_op jit(solution)/shard_map/all_to_all | solution.py:448
  104.5 0.0 copy-start.4
  104.5 0.0 copy-start.5
  104.5 0.7 first_sum.1
  105.2 11.7 %all_to_all.27.refs_0_ = bf16[8,128,128]{2,1,0:T(8,128)(2,1)S(1)} all-to-all(bf16[8,128,128]{2,1,0:T(8,128)(2,1)S(1)} %first_sum.1), channel_id=1, replica_groups={{0,16,32,48,64,80,96,112},{128,144,160,176,192,208,224,240},{256,272,28..., dimensions={0} | all-to-all | bytes 524288 | tf_op jit(solution)/shard_map/all_to_all | solution.py:448
  117.0 0.5 second_sum.1
  117.5 14.0 %all_to_all.28 = bf16[16,16,128]{2,1,0:T(8,128)(2,1)S(1)} all-to-all(bf16[16,16,128]{2,1,0:T(8,128)(2,1)S(1)} %bitcast.28), channel_id=1, replica_groups=mesh['y'=8,'x'=8,'expert'=16] {'expert'}, dimensions={0} | all-to-all | bytes 131072 | tf_op jit(solution)/shard_map/all_to_all | solution.py:437
  131.5 0.0 copy-done.4
  131.5 0.0 copy-done.5
  131.5 0.9 combine.1
Async XLA Ops:
  2.8 20.2 %copy-start = (bf16[1,84,6144]{2,1,0:T(8,128)(2,1)S(1)}, bf16[1,84,6144]{2,1,0:T(8,128)(2,1)}, u32[]{:S(2)}) copy-start(bf16[1,84,6144]{2,1,0:T(8,128)(2,1)} %param.11) | copy-start | bytes 3096580
  2.8 30.1 %all-to-all-start = ((bf16[16,64,128]{2,1,0:T(8,128)(2,1)}), bf16[16,64,128]{2,1,0:T(8,128)(2,1)S(1)}, u32[]{:S(2)}, u32[]{:S(2)}) async-start(bf16[16,64,128]{2,1,0:T(8,128)(2,1)} %bitcast.32), calls=%async_computation | async-start | bytes 524288 | tf_op jit(solution)/shard_map/all_to_all | solution.py:437
  23.0 1.2 copy-start.1
  24.3 1.5 %copy-start.3 = (bf16[1,16,10,6144]{3,1,2,0:T(8,128)(2,1)S(1)}, bf16[1,16,10,6144]{3,1,2,0:T(8,128)(2,1)}, u32[]{:S(2)}) copy-start(bf16[1,16,10,6144]{3,1,2,0:T(8,128)(2,1)} %param.10) | copy-start | bytes 5898244
  33.3 34.8 %copy-start.2 = (bf16[1,84,6144]{2,1,0:T(8,128)(2,1)S(1)}, bf16[1,84,6144]{2,1,0:T(8,128)(2,1)}, u32[]{:S(2)}) copy-start(bf16[1,84,6144]{2,1,0:T(8,128)(2,1)} %param.12) | copy-start | bytes 3096580
  104.5 27.0 %copy-start.4 = (bf16[160,34]{1,0:T(8,128)(2,1)S(1)}, bf16[160,34]{1,0:T(8,128)(2,1)}, u32[]{:S(2)}) copy-start(bf16[160,34]{1,0:T(8,128)(2,1)} %get-tuple-element.8.picker) | copy-start | bytes 32644
  104.5 27.0 %copy-start.5 = (s32[34,4]{0,1:T(4,128)S(1)}, s32[34,4]{0,1:T(4,128)}, u32[]{:S(2)}) copy-start(s32[34,4]{0,1:T(4,128)} %param.7) | copy-start | bytes 1636

commit v8 on v7

--- a/solution.py
+++ b/solution.py
@@ -94,7 +94,7 @@
     pieces = []
     for j in range(tiles):
         columns = slice(j * LANES, (j + 1) * LANES)
-        picked = jnp.where(even, dot(hot, grad_x[:, columns]), dot(hot, grad_y[:, columns]))
+        picked = jnp.where(even, dot(hot, grad_y[:, columns]), dot(hot, grad_x[:, columns]))
         pieces.append(picked.astype(BF16))
     chunk = send.shape[0] // experts
     spare = chunk - tiles * capacity - 1
@@ -469,7 +469,7 @@
     down = w_down[0].T
 
     shards, scale = spread(recv, factors, down, width // SIDE, capacity)
-    grads = exchange_in_plane(shards, True)
+    grads = exchange_in_plane(shards, False)
     parts = slot_grads(
         expert, grads, down, factors, scale, w_gate[0], w_up[0], capacity
     )

time: 133 us -> 133 us (level)
  no operation moved by 1% of the time
where the time goes in v8:
time: 133 us; the launch traced here: 132 us
  blocking collectives  94.8 us (71%)
  starting transfers between devices  18.3 us (14%)
  Pallas kernels  8.96 us (7%)
  waiting for transfers between devices  4.99 us (4%)
  local copies, waits for them, and re-layouts  4.63 us (3%)
    all_to_all x3, blocking collectives, exchange_in_plane(): lax.all_to_all(values, ('y', 'x', 'expert'), split_axis=0, concat_axis=0,...  80.8 us
    all_to_all x1, starting transfers between devices, exchange(): lax.all_to_all(values, 'expert', split_axis=0, concat_axis=0, tiled=True)  18.3 us
    all_to_all x1, blocking collectives, exchange(): lax.all_to_all(values, 'expert', split_axis=0, concat_axis=0, tiled=True)  14 us
    all_to_all x1, waiting for transfers between devices, exchange(): lax.all_to_all(values, 'expert', split_axis=0, concat_axis=0, tiled=True)  4.99 us
    unnamed x13, local copies, waits for them, and re-layouts  4.63 us
  transfers between devices with their start and end apart: 1, of which 1 were waited for; matrix products, arithmetic and copies ran while one was open for 1% of the time, Pallas kernels for 2%

profile of v8, /device:TPU:1, one launch (start us, length us, event | category | flops | bytes accessed | tf_op | source)
XLA Modules:
  0.0 132.4 jit_solution(18233502758801226339)
XLA Ops:
  0.6 2.2 %pick.1 = (bf16[1024,128]{1,0:T(8,128)(2,1)}, bf16[160,34]{1,0:T(8,128)(2,1)}) custom-call(s32[1]{0:T(128)} %bitcast.1.refs_0_, s32[1]{0:T(128)} %bitcast.2.refs_1_, s32[1]{0:T(128)} %bitcast.3.refs_2_.refs_0_, s32[4,34]{1,0:T(4,128)} %bitcast.30, f32[4,34]{1,0:T(4,128)} %bitcast.33, bf16[34,6144]{1,0:T(8,128)(2,1)} %refs_5_.1), custom_call_target="tpu_custom_call" | custom-call | tf_op jit(solution)/shard_map/pick/pallas_call | solution.py:118
  2.8 0.0 copy-start
  2.8 18.3 %all-to-all-start = ((bf16[16,64,128]{2,1,0:T(8,128)(2,1)}), bf16[16,64,128]{2,1,0:T(8,128)(2,1)S(1)}, u32[]{:S(2)}, u32[]{:S(2)}) async-start(bf16[16,64,128]{2,1,0:T(8,128)(2,1)} %bitcast.32), calls=%async_computation | async-start | bytes 524288 | tf_op jit(solution)/shard_map/all_to_all | solution.py:437
  21.2 1.8 %copy.9 = bf16[1,84,6144]{1,2,0:T(8,128)(2,1)S(1)} copy(bf16[1,84,6144]{2,1,0:T(8,128)(2,1)} %param.13) | data formatting | bytes 2064384 | tf_op args[6]
  23.0 0.0 copy-done
  23.0 0.0 copy-start.1
  23.0 1.2 copy-done.1
  24.3 0.0 copy-start.3
  24.3 1.5 %copy-done.3 = bf16[1,16,10,6144]{3,1,2,0:T(8,128)(2,1)S(1)} copy-done((bf16[1,16,10,6144]{3,1,2,0:T(8,128)(2,1)S(1)}, bf16[1,16,10,6144]{3,1,2,0:T(8,128)(2,1)}, u32[]{:S(2)}) %copy-start.3) | copy-done | bytes 1966104
  25.8 2.1 %forward.1.refs_1_.refs_3_ = f32[3,160,84]{2,1,0:T(8,128)S(1)} custom-call(bf16[160,6144]{1,0:T(8,128)(2,1)S(1)} %bitcast.26, bf16[84,6144]{1,0:T(8,128)(2,1)S(1)} %bitcast.22, bf16[84,6144]{1,0:T(8,128)(2,1)S(1)} %bitcast.24), custom_call_target="tpu_custom_call" | custom-call | flops 330301440 | bytes 8060928 | tf_op jit(solution)/shard_map/forward/pallas_call | solution.py:206
  27.9 5.0 %all-to-all-done = bf16[16,64,128]{2,1,0:T(8,128)(2,1)S(1)} async-done(((bf16[16,64,128]{2,1,0:T(8,128)(2,1)}), bf16[16,64,128]{2,1,0:T(8,128)(2,1)S(1)}, u32[]{:S(2)}, u32[]{:S(2)}) %all-to-all-start) | async-done | bytes 262176 | tf_op jit(solution)/shard_map/all_to_all | solution.py:437
  32.9 0.4 spread.1
  33.3 0.0 copy-start.2
  33.3 34.0 %all_to_all.25.refs_1_ = bf16[8,960,128]{2,1,0:T(8,128)(2,1)S(1)} all-to-all(bf16[8,960,128]{2,1,0:T(8,128)(2,1)S(1)} %get-tuple-element.10), channel_id=1, replica_groups={{0,128,256,384,512,640,768,896},{16,144,272,400,528,656,784,912},{32,16..., dimensions={0} | all-to-all | bytes 3932160 | tf_op jit(solution)/shard_map/all_to_all | solution.py:448
  67.3 0.0 copy-done.2
  67.3 2.2 %slot_grads.1 = bf16[8,976,128]{2,1,0:T(8,128)(2,1)S(1)} custom-call(s32[1]{0:T(128)} %bitcast.3.refs_2_.refs_0_, bf16[8,960,128]{2,1,0:T(8,128)(2,1)S(1)} %all_to_all.25.refs_1_, bf16[6144,84]{1,0:T(8,128)(2,1)S(1)} %bitcast.21, f32[3,160,84]{2,1,0:T(8,128)S(1)} %forward.1.refs_1_.refs_3_, f32[160,128]{1,0:T(8,128)S(1)} %get-tuple-element.11.refs_4_, ...), custom_call_target="tpu_custom_call" | custom-call | tf_op jit(solution)/shard_map/slot_grads/pallas_call | solution.py:311
  69.5 30.4 %all_to_all.26.refs_0_ = bf16[8,976,128]{2,1,0:T(8,128)(2,1)S(1)} all-to-all(bf16[8,976,128]{2,1,0:T(8,128)(2,1)S(1)} %slot_grads.1), channel_id=1, replica_groups={{0,128,256,384,512,640,768,896},{16,144,272,400,528,656,784,912},{32,16..., dimensions={0} | all-to-all | bytes 3997696 | tf_op jit(solution)/shard_map/all_to_all | solution.py:448
  99.9 0.0 copy-start.4
  99.9 0.0 copy-start.5
  99.9 0.7 first_sum.1
  100.6 16.4 %all_to_all.27.refs_0_ = bf16[8,128,128]{2,1,0:T(8,128)(2,1)S(1)} all-to-all(bf16[8,128,128]{2,1,0:T(8,128)(2,1)S(1)} %first_sum.1), channel_id=1, replica_groups={{0,16,32,48,64,80,96,112},{128,144,160,176,192,208,224,240},{256,272,28..., dimensions={0} | all-to-all | bytes 524288 | tf_op jit(solution)/shard_map/all_to_all | solution.py:448
  117.0 0.5 second_sum.1
  117.5 14.0 %all_to_all.28 = bf16[16,16,128]{2,1,0:T(8,128)(2,1)S(1)} all-to-all(bf16[16,16,128]{2,1,0:T(8,128)(2,1)S(1)} %bitcast.28), channel_id=1, replica_groups=mesh['y'=8,'x'=8,'expert'=16] {'expert'}, dimensions={0} | all-to-all | bytes 131072 | tf_op jit(solution)/shard_map/all_to_all | solution.py:437
  131.5 0.0 copy-done.4
  131.5 0.0 copy-done.5
  131.5 0.9 combine.1
Async XLA Ops:
  2.8 20.2 %copy-start = (bf16[1,84,6144]{2,1,0:T(8,128)(2,1)S(1)}, bf16[1,84,6144]{2,1,0:T(8,128)(2,1)}, u32[]{:S(2)}) copy-start(bf16[1,84,6144]{2,1,0:T(8,128)(2,1)} %param.11) | copy-start | bytes 3096580
  2.8 30.1 %all-to-all-start = ((bf16[16,64,128]{2,1,0:T(8,128)(2,1)}), bf16[16,64,128]{2,1,0:T(8,128)(2,1)S(1)}, u32[]{:S(2)}, u32[]{:S(2)}) async-start(bf16[16,64,128]{2,1,0:T(8,128)(2,1)} %bitcast.32), calls=%async_computation | async-start | bytes 524288 | tf_op jit(solution)/shard_map/all_to_all | solution.py:437
  23.0 1.2 copy-start.1
  24.3 1.5 %copy-start.3 = (bf16[1,16,10,6144]{3,1,2,0:T(8,128)(2,1)S(1)}, bf16[1,16,10,6144]{3,1,2,0:T(8,128)(2,1)}, u32[]{:S(2)}) copy-start(bf16[1,16,10,6144]{3,1,2,0:T(8,128)(2,1)} %param.10) | copy-start | bytes 5898244
  33.3 34.0 %copy-start.2 = (bf16[1,84,6144]{2,1,0:T(8,128)(2,1)S(1)}, bf16[1,84,6144]{2,1,0:T(8,128)(2,1)}, u32[]{:S(2)}) copy-start(bf16[1,84,6144]{2,1,0:T(8,128)(2,1)} %param.12) | copy-start | bytes 3096580
  99.9 31.7 %copy-start.4 = (bf16[160,34]{1,0:T(8,128)(2,1)S(1)}, bf16[160,34]{1,0:T(8,128)(2,1)}, u32[]{:S(2)}) copy-start(bf16[160,34]{1,0:T(8,128)(2,1)} %get-tuple-element.8.picker) | copy-start | bytes 32644
  99.9 31.7 %copy-start.5 = (s32[34,4]{0,1:T(4,128)S(1)}, s32[34,4]{0,1:T(4,128)}, u32[]{:S(2)}) copy-start(s32[34,4]{0,1:T(4,128)} %param.7) | copy-start | bytes 1636
